TPU v7x, 128 devices: a whole 4x4x4 slice. The times are simulated.
128 devices in a mesh: fsdp: 8 (over y, core), expert: 16 (over z, x).
Axes of the slice: x: 4, y: 4, z: 4, core: 2. Of those that a mesh axis runs over, the one named last changes fastest.
Arguments:
- hidden_in: bfloat16 [16, 1280, 1024], P('expert', 'fsdp'), may hold values from -6 to 6
- grad_out: bfloat16 [16, 1280, 1024], P('expert', 'fsdp'), may hold values from -6 to 6
- lengths: int32 [16, 3], P('expert'), may hold values from 1 to 1278, as said below
- experts: int32 [16, 1280, 8], P('expert', 'fsdp'), may hold values from 0 to 31, all different within a row; in each aligned block of 160 rows (0 to 159, 160 to 319, ..., all dimensions but the last counted through in order) at most 50 rows name the same one
- gain_attn: bfloat16 [1024], P('fsdp'), may hold values from 0.5 to 1.5
- w_query: bfloat16 [1024, 1024], P('fsdp'), may hold values from -0.1875 to 0.1875
- key_weight: bfloat16 [1024, 512], P('fsdp'), may hold values from -0.1875 to 0.1875
- value_weight: bfloat16 [1024, 512], P('fsdp'), may hold values from -0.1875 to 0.1875
- w_out: bfloat16 [1024, 1024], P('fsdp'), may hold values from -0.75 to 0.75
- gain_moe: bfloat16 [1024], P('fsdp'), may hold values from 0.5 to 1.5
- w_router: bfloat16 [1024, 32], P('fsdp'), may hold values from -0.09375 to 0.09375
- expert_gate: bfloat16 [32, 1024, 512], P('expert', 'fsdp'), may hold values from -0.1875 to 0.1875
- expert_up: bfloat16 [32, 1024, 512], P('expert', 'fsdp'), may hold values from -0.1875 to 0.1875
- expert_down: bfloat16 [32, 512, 1024], P('expert', 'fsdp'), may hold values from -1 to 1
Outputs:
- hidden_out: bfloat16 [16, 1280, 1024], P('expert', 'fsdp')
- grad_hidden_in: bfloat16 [16, 1280, 1024], P('expert', 'fsdp')
- grad_gain_attn: float32 [1024], P('fsdp')
- grad_w_query: float32 [1024, 1024], P('fsdp')
- grad_w_key: float32 [1024, 512], P('fsdp')
- grad_w_value: float32 [1024, 512], P('fsdp')
- grad_w_out: float32 [1024, 1024], P('fsdp')
- grad_gain_moe: float32 [1024], P('fsdp')
- grad_w_router: float32 [1024, 32], P('fsdp')
- grad_expert_gate: float32 [32, 1024, 512], P('expert', 'fsdp')
- grad_expert_up: float32 [32, 1024, 512], P('expert', 'fsdp')
- grad_expert_down: float32 [32, 512, 1024], P('expert', 'fsdp')
Inputs may be any that keep to these rules, and one draw needn't show every extreme that they name: In each pack the 3 lengths add up to 1280; one of them, at a place drawn from the seed, begins within the first 160 tokens and ends within the last 160; in the first pack every other length is 1. Each token names 8 different experts; among the rows of one device no expert is named more than 50 times, a bound that some block reaches.
All inputs are finite; a program needn't handle non-finite values.
Results may differ from a plain program's by a relative error of at most 0.028.
Values may be sent and summed in bfloat16 or wider, within the bound.
A program may use at most 192 MiB of HBM per device.

v0:
```python
import math

import jax
import jax.numpy as jnp
from jax import lax
from jax.sharding import PartitionSpec as P

QUERY_HEADS = 16
KEY_VALUE_HEADS = 8
HEAD_SIZE = 64
TOPK = 8


EPS = 1e-06
BASE = 10000.0


def sent_together(arrays, axis, dim, along):
    widths = [math.prod(a.shape[along:]) for a in arrays]
    both = jnp.concatenate(
        [a.reshape(*a.shape[:along], w) for a, w in zip(arrays, widths)], axis=along
    )
    result = lax.all_gather(both, axis, axis=dim, tiled=True)
    blocks = jnp.split(result, [sum(widths[:k]) for k in range(1, len(widths))], axis=along)
    return tuple(
        (b.reshape(*result.shape[:along], *a.shape[along:]) for a, b in zip(arrays, blocks))
    )


def sent_together_2(arrays, axis, dim, along):
    ends, at = ([], 0)
    for a in arrays[:-1]:
        at += a.shape[along]
        ends.append(at)
    both = jnp.concatenate(arrays, axis=along)
    return tuple(jnp.split(lax.all_gather(both, axis, axis=dim, tiled=True), ends, axis=along))


def sent_together_3(arrays, axis, dim, along):
    ends, at = ([], 0)
    for a in arrays[:-1]:
        at += a.shape[along]
        ends.append(at)
    both = jnp.concatenate(arrays, axis=along)
    return tuple(
        jnp.split(lax.psum_scatter(both, axis, scatter_dimension=dim, tiled=True), ends, axis=along)
    )


def side_by_side(arrays, axis, dim, along):
    widths = [math.prod(a.shape[along:]) for a in arrays]
    both = jnp.concatenate(
        [a.reshape(*a.shape[:along], w) for a, w in zip(arrays, widths)], axis=along
    )
    result = lax.psum_scatter(both, axis, scatter_dimension=dim, tiled=True)
    blocks = jnp.split(result, [sum(widths[:k]) for k in range(1, len(widths))], axis=along)
    return tuple(
        (b.reshape(*result.shape[:along], *a.shape[along:]) for a, b in zip(arrays, blocks))
    )


def contract_first(left_op, right_op):
    return lax.dot_general(
        left_op, right_op, (((0,), (0,)), ((), ())), preferred_element_type=jnp.float32
    )


def contract_last(left_op, right_op):
    return lax.dot_general(
        left_op, right_op, (((1,), (1,)), ((), ())), preferred_element_type=jnp.float32
    )


def rotary(offset):
    half_dim = HEAD_SIZE // 2
    frequency = BASE ** (-2.0 * jnp.arange(half_dim, dtype=jnp.float32) / HEAD_SIZE)
    angles = offset.astype(jnp.float32)[:, None] * frequency[None, :]
    angles = jnp.concatenate([angles, angles], axis=1)
    return (jnp.cos(angles), jnp.sin(angles))


def apply_rotation(vector, cosine_table, sine_lookup, direction):
    half_dim = HEAD_SIZE // 2
    swapped = jnp.concatenate([-vector[..., half_dim:], vector[..., :half_dim]], axis=-1)
    return vector * cosine_table[:, None, :] + direction * swapped * sine_lookup[:, None, :]


def norm_back(inputs, inverse_rms, gain_vec, upstream):
    scaled = upstream * gain_vec
    gain_grad = jnp.sum(upstream * inputs * inverse_rms, axis=0)
    spread = jnp.mean(scaled * inputs, axis=-1, keepdims=True)
    return (inverse_rms * scaled - inputs * inverse_rms**3 * spread, gain_grad)


def shards(
    hidden_in,
    grad_out,
    lengths,
    experts,
    gain_attn,
    w_query,
    key_weight,
    value_weight,
    w_out,
    gain_moe,
    w_router,
    expert_gate,
    expert_up,
    expert_down,
):
    (
        full_gain_a,
        full_query,
        full_key,
        full_value,
        full_out,
        full_gain_m,
        full_router,
        full_gate,
        full_up,
        full_down,
    ) = (
        *sent_together(
            (gain_attn, w_query, key_weight, value_weight, w_out, gain_moe, w_router), "fsdp", 0, 1
        ),
        *sent_together_2((expert_gate, expert_up), "fsdp", 1, 0),
        lax.all_gather(expert_down, "fsdp", axis=1, tiled=True),
    )
    shard_count = lax.axis_size("fsdp")
    owner_count = lax.axis_size("expert")
    shard_index = lax.axis_index("fsdp")
    resident_rows = hidden_in.shape[1]
    model_width = hidden_in.shape[2]
    packed_length = resident_rows * shard_count
    expert_count = full_router.shape[1]
    per_owner = full_gate.shape[0]
    capacity = max(3, 5 * resident_rows * TOPK // (4 * expert_count))
    query_group_width = QUERY_HEADS // KEY_VALUE_HEADS
    score_scale = HEAD_SIZE ** (-0.5)
    inputs = hidden_in[0].astype(jnp.float32)
    upstream = grad_out[0].astype(jnp.float32)
    picked_ids = experts[0]
    seq_lengths = lengths[0]
    seq_ends = jnp.cumsum(seq_lengths, dtype=jnp.int32)
    starts = seq_ends - seq_lengths
    token_index = jnp.arange(packed_length, dtype=jnp.int32)[:, None]
    inside = ((token_index >= starts[None, :]) & (token_index < seq_ends[None, :])).astype(
        jnp.int32
    )
    segment = jnp.sum(inside * jnp.arange(seq_lengths.shape[0], dtype=jnp.int32)[None, :], axis=1)
    offset = jnp.sum(inside * (token_index - starts[None, :]), axis=1)
    first_row = shard_index * resident_rows
    own_segment = lax.dynamic_slice_in_dim(segment, first_row, resident_rows)
    own_offset = lax.dynamic_slice_in_dim(offset, first_row, resident_rows)
    cosine_table, sine_lookup = rotary(own_offset)
    position = first_row + jnp.arange(resident_rows, dtype=jnp.int32)
    allowed = (own_segment[:, None] == segment[None, :]) & (
        jnp.arange(packed_length, dtype=jnp.int32)[None, :] <= position[:, None]
    )
    inverse_a = lax.rsqrt(jnp.mean(inputs * inputs, axis=-1, keepdims=True) + EPS)
    rescaled_hidden = (inputs * inverse_a * full_gain_a).astype(jnp.bfloat16)
    query_rows = jnp.dot(rescaled_hidden, full_query, preferred_element_type=jnp.float32).reshape(
        resident_rows, QUERY_HEADS, HEAD_SIZE
    )
    key_row_block = jnp.dot(rescaled_hidden, full_key, preferred_element_type=jnp.float32).reshape(
        resident_rows, KEY_VALUE_HEADS, HEAD_SIZE
    )
    value_rows = jnp.dot(rescaled_hidden, full_value, preferred_element_type=jnp.float32).astype(
        jnp.bfloat16
    )
    query_rows = (
        apply_rotation(query_rows, cosine_table, sine_lookup, 1.0)
        .astype(jnp.bfloat16)
        .reshape(resident_rows, KEY_VALUE_HEADS, query_group_width, HEAD_SIZE)
    )
    key_row_block = (
        apply_rotation(key_row_block, cosine_table, sine_lookup, 1.0)
        .astype(jnp.bfloat16)
        .reshape(resident_rows, KEY_VALUE_HEADS * HEAD_SIZE)
    )
    gathered_keys, gathered_values = sent_together_2((key_row_block, value_rows), "fsdp", 0, 1)
    gathered_keys = gathered_keys.reshape(packed_length, KEY_VALUE_HEADS, HEAD_SIZE)
    gathered_values = gathered_values.reshape(packed_length, KEY_VALUE_HEADS, HEAD_SIZE)

    def attend_scores():
        raw_scores = jnp.einsum(
            "qhgd,khd->hgqk", query_rows, gathered_keys, preferred_element_type=jnp.float32
        )
        return jnp.where(allowed, raw_scores * score_scale, -1e30)

    scores = attend_scores()
    row_top = jnp.max(scores, axis=-1, keepdims=True)
    row_total = jnp.sum(jnp.exp(scores - row_top), axis=-1, keepdims=True)
    weights_low = (jnp.exp(scores - row_top) / row_total).astype(jnp.bfloat16)
    attended = jnp.einsum(
        "hgqk,khd->qhgd", weights_low, gathered_values, preferred_element_type=jnp.float32
    )
    attended_low = attended.reshape(resident_rows, QUERY_HEADS * HEAD_SIZE).astype(jnp.bfloat16)
    hidden = inputs + jnp.dot(attended_low, full_out, preferred_element_type=jnp.float32)
    inverse_m = lax.rsqrt(jnp.mean(hidden * hidden, axis=-1, keepdims=True) + EPS)
    routed = (hidden * inverse_m * full_gain_m).astype(jnp.bfloat16)
    logits = jnp.dot(routed, full_router, preferred_element_type=jnp.float32)
    onehot = picked_ids[:, :, None] == jnp.arange(expert_count, dtype=jnp.int32)[None, None, :]
    chosen = jnp.sum(jnp.where(onehot, logits[:, None, :], 0.0), axis=-1)
    gate_probs = jax.nn.softmax(chosen, axis=-1)
    flat_ids = picked_ids.reshape(resident_rows * TOPK)
    flat_hot = (flat_ids[:, None] == jnp.arange(expert_count, dtype=jnp.int32)[None, :]).astype(
        jnp.int32
    )
    counted = jnp.cumsum(flat_hot, axis=0, dtype=jnp.int32)
    slot_index = jnp.sum(counted * flat_hot, axis=1) - 1
    targets = flat_ids * capacity + slot_index
    outgoing = jnp.zeros((expert_count * capacity, model_width), jnp.bfloat16)
    outgoing = (
        outgoing.at[targets]
        .set(jnp.repeat(routed, TOPK, axis=0))
        .reshape(owner_count, per_owner, capacity, model_width)
    )
    arrived = lax.all_to_all(outgoing, "expert", split_axis=0, concat_axis=0, tiled=True)
    gate_part = jnp.einsum("sxcd,xdf->sxcf", arrived, full_gate, preferred_element_type=jnp.float32)
    up_part = jnp.einsum("sxcd,xdf->sxcf", arrived, full_up, preferred_element_type=jnp.float32)
    inner_act = (jax.nn.silu(gate_part) * up_part).astype(jnp.bfloat16)
    produced = jnp.einsum(
        "sxcf,xfd->sxcd", inner_act, full_down, preferred_element_type=jnp.float32
    ).astype(jnp.bfloat16)
    returned = lax.all_to_all(produced, "expert", split_axis=0, concat_axis=0, tiled=True)
    gathered_back = returned.reshape(expert_count * capacity, model_width)[targets].reshape(
        resident_rows, TOPK, model_width
    )
    output = hidden + jnp.sum(gate_probs[:, :, None] * gathered_back.astype(jnp.float32), axis=1)
    grad_gates = jnp.sum(gathered_back.astype(jnp.float32) * upstream[:, None, :], axis=-1)
    grad_pairs = (
        (gate_probs[:, :, None] * upstream[:, None, :])
        .astype(jnp.bfloat16)
        .reshape(resident_rows * TOPK, model_width)
    )
    grad_outgoing = jnp.zeros((expert_count * capacity, model_width), jnp.bfloat16)
    grad_outgoing = (
        grad_outgoing.at[targets]
        .set(grad_pairs)
        .reshape(owner_count, per_owner, capacity, model_width)
    )
    grad_arrived = lax.all_to_all(grad_outgoing, "expert", split_axis=0, concat_axis=0, tiled=True)
    grad_inner = jnp.einsum(
        "sxcd,xfd->sxcf", grad_arrived, full_down, preferred_element_type=jnp.float32
    )
    grad_down_w = jnp.einsum(
        "sxcf,sxcd->xfd", inner_act, grad_arrived, preferred_element_type=jnp.float32
    )
    sigmoid_gate = jax.nn.sigmoid(gate_part)
    grad_gate_part = (
        grad_inner * up_part * sigmoid_gate * (1.0 + gate_part * (1.0 - sigmoid_gate))
    ).astype(jnp.bfloat16)
    grad_up_part = (grad_inner * gate_part * sigmoid_gate).astype(jnp.bfloat16)
    grad_rows = jnp.einsum(
        "sxcf,xdf->sxcd", grad_gate_part, full_gate, preferred_element_type=jnp.float32
    )
    grad_rows = (
        grad_rows
        + jnp.einsum("sxcf,xdf->sxcd", grad_up_part, full_up, preferred_element_type=jnp.float32)
    ).astype(jnp.bfloat16)
    grad_gate_w = jnp.einsum(
        "sxcd,sxcf->xdf", arrived, grad_gate_part, preferred_element_type=jnp.float32
    )
    grad_up_w = jnp.einsum(
        "sxcd,sxcf->xdf", arrived, grad_up_part, preferred_element_type=jnp.float32
    )
    grad_returned = lax.all_to_all(grad_rows, "expert", split_axis=0, concat_axis=0, tiled=True)
    grad_routed = jnp.sum(
        grad_returned.reshape(expert_count * capacity, model_width)[targets]
        .reshape(resident_rows, TOPK, model_width)
        .astype(jnp.float32),
        axis=1,
    )
    grad_chosen = gate_probs * (
        grad_gates - jnp.sum(gate_probs * grad_gates, axis=-1, keepdims=True)
    )
    grad_logits = jnp.sum(jnp.where(onehot, grad_chosen[:, :, None], 0.0), axis=1).astype(
        jnp.bfloat16
    )
    grad_routed = grad_routed + contract_last(grad_logits, full_router)
    grad_router_w = contract_first(routed, grad_logits)
    grad_middle, grad_gain_m = norm_back(hidden, inverse_m, full_gain_m, grad_routed)
    grad_hidden = upstream + grad_middle
    grad_hidden_low = grad_hidden.astype(jnp.bfloat16)
    grad_out_w = contract_first(attended_low, grad_hidden_low)
    grad_attended = (
        contract_last(grad_hidden_low, full_out)
        .astype(jnp.bfloat16)
        .reshape(resident_rows, KEY_VALUE_HEADS, query_group_width, HEAD_SIZE)
    )
    scores = attend_scores()
    weights_soft = jnp.exp(scores - row_top) / row_total
    grad_weights = jnp.einsum(
        "qhgd,khd->hgqk", grad_attended, gathered_values, preferred_element_type=jnp.float32
    )
    grad_scores = (
        weights_soft
        * (grad_weights - jnp.sum(weights_soft * grad_weights, axis=-1, keepdims=True))
        * score_scale
    ).astype(jnp.bfloat16)
    grad_queries = jnp.einsum(
        "hgqk,khd->qhgd", grad_scores, gathered_keys, preferred_element_type=jnp.float32
    ).reshape(resident_rows, QUERY_HEADS, HEAD_SIZE)
    grad_keys_part = jnp.einsum(
        "hgqk,qhgd->khd", grad_scores, query_rows, preferred_element_type=jnp.float32
    ).reshape(packed_length, KEY_VALUE_HEADS * HEAD_SIZE)
    grad_values_part = jnp.einsum(
        "hgqk,qhgd->khd",
        weights_soft.astype(jnp.bfloat16),
        grad_attended,
        preferred_element_type=jnp.float32,
    ).reshape(packed_length, KEY_VALUE_HEADS * HEAD_SIZE)
    key_gradient, grad_values = tuple(
        (
            part.astype(jnp.float32)
            for part in sent_together_3(
                (grad_keys_part.astype(jnp.bfloat16), grad_values_part.astype(jnp.bfloat16)),
                "fsdp",
                0,
                1,
            )
        )
    )
    grad_queries = (
        apply_rotation(grad_queries, cosine_table, sine_lookup, -1.0)
        .astype(jnp.bfloat16)
        .reshape(resident_rows, QUERY_HEADS * HEAD_SIZE)
    )
    key_gradient = (
        apply_rotation(
            key_gradient.reshape(resident_rows, KEY_VALUE_HEADS, HEAD_SIZE),
            cosine_table,
            sine_lookup,
            -1.0,
        )
        .astype(jnp.bfloat16)
        .reshape(resident_rows, KEY_VALUE_HEADS * HEAD_SIZE)
    )
    grad_values = grad_values.astype(jnp.bfloat16)
    grad_query_w = contract_first(rescaled_hidden, grad_queries)
    grad_key_w = contract_first(rescaled_hidden, key_gradient)
    grad_value_w = contract_first(rescaled_hidden, grad_values)
    grad_normed = (
        contract_last(grad_queries, full_query)
        + contract_last(key_gradient, full_key)
        + contract_last(grad_values, full_value)
    )
    grad_first, grad_gain_a = norm_back(inputs, inverse_a, full_gain_a, grad_normed)
    grad_input = (grad_hidden + grad_first).astype(jnp.bfloat16)
    (
        sum_gain_a,
        sum_query,
        sum_key,
        sum_value,
        sum_out,
        sum_gain_m,
        sum_router,
        sum_gate,
        sum_up,
        sum_down,
    ) = (
        *tuple(
            (
                part.astype(jnp.float32)
                for part in side_by_side(
                    (
                        grad_gain_a.astype(jnp.bfloat16),
                        grad_query_w.astype(jnp.bfloat16),
                        grad_key_w.astype(jnp.bfloat16),
                        grad_value_w.astype(jnp.bfloat16),
                        grad_out_w.astype(jnp.bfloat16),
                        grad_gain_m.astype(jnp.bfloat16),
                        grad_router_w.astype(jnp.bfloat16),
                    ),
                    "fsdp",
                    0,
                    1,
                )
            )
        ),
        *tuple(
            (
                part.astype(jnp.float32)
                for part in sent_together_3(
                    (grad_gate_w.astype(jnp.bfloat16), grad_up_w.astype(jnp.bfloat16)), "fsdp", 1, 0
                )
            )
        ),
        lax.psum_scatter(
            grad_down_w.astype(jnp.bfloat16), "fsdp", scatter_dimension=1, tiled=True
        ).astype(jnp.float32),
    )
    tot_gain_a, tot_query, tot_key, tot_value, tot_out, tot_gain_m, tot_router = (
        lax.psum(sum_gain_a.astype(jnp.bfloat16), "expert").astype(jnp.float32),
        lax.psum(sum_query.astype(jnp.bfloat16), "expert").astype(jnp.float32),
        lax.psum(sum_key.astype(jnp.bfloat16), "expert").astype(jnp.float32),
        lax.psum(sum_value.astype(jnp.bfloat16), "expert").astype(jnp.float32),
        lax.psum(sum_out.astype(jnp.bfloat16), "expert").astype(jnp.float32),
        lax.psum(sum_gain_m.astype(jnp.bfloat16), "expert").astype(jnp.float32),
        lax.psum(sum_router.astype(jnp.bfloat16), "expert").astype(jnp.float32),
    )
    return (
        output.astype(jnp.bfloat16)[None],
        grad_input[None],
        tot_gain_a,
        tot_query,
        tot_key,
        tot_value,
        tot_out,
        tot_gain_m,
        tot_router,
        sum_gate,
        sum_up,
        sum_down,
    )


def solution(mesh):
    placed = (
        P("expert", "fsdp", None),
        P("expert", "fsdp", None),
        P("expert", None),
        P("expert", "fsdp", None),
        P("fsdp"),
        P("fsdp", None),
        P("fsdp", None),
        P("fsdp", None),
        P("fsdp", None),
        P("fsdp"),
        P("fsdp", None),
        P("expert", "fsdp", None),
        P("expert", "fsdp", None),
        P("expert", "fsdp", None),
    )
    return jax.shard_map(
        shards,
        mesh=mesh,
        in_specs=placed,
        out_specs=(
            P("expert", "fsdp", None),
            P("expert", "fsdp", None),
            P("fsdp"),
            P("fsdp", None),
            P("fsdp", None),
            P("fsdp", None),
            P("fsdp", None),
            P("fsdp"),
            P("fsdp", None),
            P("expert", "fsdp", None),
            P("expert", "fsdp", None),
            P("expert", "fsdp", None),
        ),
        check_vma=False,
    )
```

profile of v0, /device:TPU:0, one launch (start us, length us, event | category | flops | bytes accessed | tf_op | source)
XLA Modules:
  0.0 724.3 jit_solution(17059927929994550264)
XLA Ops:
  9.6 2.5 concatenate.43
  16.4 40.4 %all-gather.5.cloned.1.call-done = bf16[1024,3106]{1,0:T(8,128)(2,1)} async-done(((bf16[128,3106]{1,0:T(8,128)(2,1)}), bf16[1024,3106]{1,0:T(8,128)(2,1)}) %all-gather.5.cloned.1.call-update) | async-done | bytes 6361104 | tf_op jit(solution)/shard_map/all_gather | solution.py:23
  61.4 1.9 convolution_convert_fusion.4
  65.7 9.2 %reduce-window.11 = s32[32,10,128]{2,1,0:T(8,128)S(1)} reduce-window(s32[32,10,128]{2,1,0:T(8,128)S(1)} %fusion.130, s32[]{:T(128)} %constant.22.clone.1), window={size=1x1x128 pad=0_0x0_0x127_0}, to_apply=%region_10.11 | reduce-window | flops 5201920 | bytes 327684 | tf_op jit(solution)/shard_map/reduce-window.1
  76.6 2.7 slice_bitcast_fusion.2
  79.3 2.6 copy.139
  81.9 2.4 fusion.125
  84.7 5.7 all-gather.7.cloned.1.call-done
  94.4 11.2 %fusion.165 = (f32[8,2,160]{2,1,0:T(2,128)S(1)}, f32[8,2,160,1280]{3,2,1,0:T(8,128)}) fusion(pred[160,1280]{1,0:T(8,128)(4,1)} %fusion.102, bf16[1280,8,64,1]{0,2,3,1:T(8,128)(2,1)} %bitcast.322, bf16[160,8,2,64]{0,3,2,1:T(8,128)(2,1)S(1)} %bitcast.327), kind=kOutput, calls=%fused_computation.234 | convolution fusion | flops 432538880 | bytes 14960640 | tf_op jit(solution)/shard_map/sub | solution.py:194
  105.6 7.1 fusion.76
  112.7 3.1 multiply_reduce_fusion.2
  117.6 10.0 %scatter_custom_fusion = bf16[1600,1024]{1,0:T(8,128)(2,1)S(1)} fusion(s32[1280]{0:T(1024)S(1)} %fusion.147, bf16[]{:T(256)} %constant.56.clone.1, bf16[160,1024]{1,0:T(8,128)(2,1)} %multiply_convert_fusion), kind=kCustom, calls=%fused_computation.73 | custom fusion | bytes 3604482 | tf_op jit(solution)/shard_map/scatter | solution.py:216
  127.6 2.7 reshape.471
  130.2 7.1 copy.146
  137.4 7.1 all-to-all-start
  147.7 14.5 %scatter_custom_fusion.1 = bf16[1600,1024]{1,0:T(8,128)(2,1)S(1)} fusion(s32[1280]{0:T(1024)S(1)} %fusion.147, f32[160,1024]{1,0:T(8,128)} %bitcast_convert_fusion.3, f32[1280]{0:T(1024)S(1)} %div.63, bf16[]{:T(256)} %constant.56.clone.1), kind=kCustom, calls=%fused_computation.71 | custom fusion | flops 2621440 | bytes 3940354 | tf_op jit(solution)/shard_map/scatter | solution.py:240
  162.2 2.7 reshape.473
  164.9 7.2 copy.152
  172.0 23.0 %all-to-all-done = bf16[16,2,50,1024]{3,1,2,0:T(2,128)(2,1)} async-done(((bf16[16,2,50,1024]{3,1,2,0:T(2,128)(2,1)}), bf16[16,2,50,1024]{3,1,2,0:T(2,128)(2,1)}, u32[]{:S(2)}, u32[]{:S(2)}) %all-to-all-start) | async-done | bytes 3276832 | tf_op jit(solution)/shard_map/all_to_all | solution.py:219
  195.0 4.7 all-to-all-start.2
  199.8 6.6 fusion.46
  206.4 5.8 fusion.48
  212.1 35.0 %all-to-all-done.2 = bf16[16,2,50,1024]{3,1,2,0:T(2,128)(2,1)S(1)} async-done(((bf16[16,2,50,1024]{3,1,2,0:T(2,128)(2,1)}), bf16[16,2,50,1024]{3,1,2,0:T(2,128)(2,1)S(1)}, u32[]{:S(2)}, u32[]{:S(2)}) %all-to-all-start.2) | async-done | bytes 3276832 | tf_op jit(solution)/shard_map/all_to_all | solution.py:243
  247.1 9.1 %fusion.20 = (bf16[16,2,50,512]{3,2,0,1:T(8,128)(2,1)}, bf16[16,2,50,512]{3,2,0,1:T(8,128)(2,1)}, bf16[16,2,50,512]{3,2,0,1:T(8,128)(2,1)S(1)}) fusion(f32[2,512,16,50]{1,3,2,0:T(8,128)} %fusion.48, f32[2,512,16,50]{1,3,2,0:T(8,128)} %fusion.46, bf16[2,512,1024]{2,1,0:T(8,128)(2,1)} %all-gather.11.cloned.1.call-done, ...), kind=kOutput, calls=%fused_computation.40 | convolution fusion | flops 1690828800 | bytes 16842752 | tf_op jit(solution)/shard_map/sxcd,xfd->sxcf/dot_general | solution.py:244
  257.5 2.1 convert_bitcast_fusion
  259.6 5.1 copy.149
  264.7 4.0 all-to-all-start.1
  268.7 4.4 fusion.74
  273.1 2.2 fusion.15
  275.3 5.1 copy.154
  280.4 32.7 %all-to-all-done.1 = bf16[16,2,50,1024]{3,1,2,0:T(2,128)(2,1)S(1)} async-done(((bf16[16,2,50,1024]{3,1,2,0:T(2,128)(2,1)}), bf16[16,2,50,1024]{3,1,2,0:T(2,128)(2,1)S(1)}, u32[]{:S(2)}, u32[]{:S(2)}) %all-to-all-start.1) | async-done | bytes 3276832 | tf_op jit(solution)/shard_map/all_to_all | solution.py:226
  313.1 4.5 all-to-all-start.3
  317.6 3.0 copy.150
  320.6 3.5 reshape.472
  324.2 5.1 gather_fusion
  329.3 4.7 fusion.11
  334.2 28.4 %all-to-all-done.3 = bf16[16,2,50,1024]{3,1,2,0:T(2,128)(2,1)} async-done(((bf16[16,2,50,1024]{3,1,2,0:T(2,128)(2,1)}), bf16[16,2,50,1024]{3,1,2,0:T(2,128)(2,1)}, u32[]{:S(2)}, u32[]{:S(2)}) %all-to-all-start.3) | async-done | bytes 3276832 | tf_op jit(solution)/shard_map/all_to_all | solution.py:268
  362.5 4.9 copy.155
  367.4 3.2 reshape.474
  370.6 5.1 gather_fusion.1
  375.7 3.7 convert_reduce_fusion
  381.9 2.7 fusion.88
  384.8 7.5 %fusion.39 = bf16[8,64,1280]{2,1,0:T(8,128)(2,1)} fusion(bf16[160,8,2,64]{0,3,2,1:T(8,128)(2,1)S(1)} %bitcast.314, f32[8,2,160,1280]{3,2,1,0:T(8,128)} %get-tuple-element.120, f32[8,2,160]{2,1,0:T(2,128)S(1)} %get-tuple-element.119), kind=kOutput, calls=%fused_computation.62 | convolution fusion | flops 426639360 | bytes 14755840 | tf_op jit(solution)/shard_map/hgqk,qhgd->khd/dot_general | solution.py:308
  392.4 6.6 fusion.166
  399.0 31.8 %fusion.38 = bf16[8,64,1280]{2,1,0:T(8,128)(2,1)} fusion(bf16[160,8,2,64]{0,3,2,1:T(8,128)(2,1)S(1)} %bitcast.328, f32[8,1280,160,2]{1,2,3,0:T(8,128)} %fusion.166, f32[8,2,160,1280]{3,2,1,0:T(8,128)} %get-tuple-element.120, f32[8,2,160]{2,1,0:T(2,128)S(1)} %get-tuple-element.119), kind=kOutput, calls=%fused_computation.61 | convolution fusion | flops 443027200 | bytes 27863040 | tf_op jit(solution)/shard_map/hgqk,qhgd->khd/dot_general | solution.py:305
  430.8 1.9 pad_maximum_fusion.1
  432.7 2.8 copy.176
  435.6 6.4 bitcast_convert_fusion
  442.0 30.8 %fusion.14 = f32[8,64,2,160]{3,1,2,0:T(8,128)S(1)} fusion(bf16[1280,8,64,1]{0,2,3,1:T(8,128)(2,1)} %bitcast.323, f32[8,1280,160,2]{1,2,3,0:T(8,128)} %fusion.166, f32[8,2,160,1280]{3,2,1,0:T(8,128)} %get-tuple-element.120, f32[8,2,160]{2,1,0:T(2,128)S(1)} %get-tuple-element.119), kind=kOutput, calls=%fused_computation.28 | convolution fusion | flops 442371840 | bytes 28190720 | tf_op jit(solution)/shard_map/hgqk,khd->qhgd/dot_general | solution.py:302
  475.8 2.2 convolution_convert_fusion.1
  481.7 1.9 fusion.97
  483.6 2.1 fusion.100
  485.7 4.2 fusion.117
  492.9 36.9 %concatenate.53 = bf16[1024,3106]{0,1:T(8,128)(2,1)} concatenate(bf16[1024,1]{0,1:T(2,128)(2,1)S(1)} %convert_element_type.327, bf16[1024,1024]{0,1:T(8,128)(2,1)S(1)} %convolution_convert_fusion, bf16[1024,512]{0,1:T(8,128)(2,1)} %convolution_convert_fusion.3, bf16[1024,512]{0,1:T(8,128)(2,1)} %convolution_convert_fusion.2, bf16[1024,1024]{0,1:T(8,128)(2,1)} %convolution_convert_fusion.1, ...), dimensions={1} | concatenate | bytes 12722176 | tf_op jit(solution)/shard_map/concatenate | solution.py:52
  529.8 9.1 %copy.178 = bf16[1024,3106]{1,0:T(8,128)(2,1)} copy(bf16[1024,3106]{0,1:T(8,128)(2,1)} %concatenate.53) | data formatting | bytes 12722176
  540.4 4.7 bitcast_convert_fusion.1
  545.1 4.9 bitcast_convert_fusion.2
  550.0 2.4 pad_maximum_fusion
  554.4 26.4 %reduce-scatter.15.cloned.1.call-done = bf16[128,3106]{1,0:T(8,128)(2,1)} async-done(((bf16[1024,3106]{1,0:T(8,128)(2,1)}), bf16[128,3106]{1,0:T(8,128)(2,1)}) %reduce-scatter.15.cloned.1.call-update) | async-done | bytes 795152
  587.4 33.2 %reduce-scatter.9.cloned.1.call-done = bf16[4,128,512]{2,1,0:T(8,128)(2,1)} async-done(((bf16[4,1024,512]{2,1,0:T(8,128)(2,1)}), bf16[4,128,512]{2,1,0:T(8,128)(2,1)}) %reduce-scatter.9.cloned.1.call-update) | async-done | bytes 524304 | tf_op jit(solution)/shard_map/reduce_scatter | solution.py:46
  620.6 2.1 slice_convert_fusion
  624.7 41.8 %all-reduce = (bf16[128]{0:T(256)(128)(2,1)S(1)}, bf16[128]{0:T(256)(128)(2,1)S(1)}, bf16[128,32]{0,1:T(8,128)(2,1)S(1)}) all-reduce(bf16[128]{0:T(256)(128)(2,1)S(1)} %bitcast.334, bf16[128]{0:T(256)(128)(2,1)S(1)} %bitcast.333, bf16[128,32]{0,1:T(8,128)(2,1)S(1)} %copy.188), channel_id=1, replica_groups=mesh['fsdp'=8,'expert'=16] {'expert'}, use_global_device_ids=true, to_apply=%region_27.28 | all-reduce | flops 4352 | bytes 17408 | tf_op jit(solution)/shard_map/psum | solution.py:395
  668.1 42.3 %all-reduce.4.cloned.1.call-done = (bf16[128,1024]{0,1:T(8,128)(2,1)}, bf16[128,512]{0,1:T(8,128)(2,1)}, bf16[128,512]{0,1:T(8,128)(2,1)}, bf16[128,1024]{0,1:T(8,128)(2,1)}) async-done(((bf16[128,1024]{0,1:T(8,128)(2,1)}, bf16[128,512]{0,1:T(8,128)(2,1)}, bf16[128,512]{0,1:T(8,128)(2,1)}, bf16[128,1024]{0,1:T(8,128)(2,1)}), (bf16[128,1024]{0,1:T(8,128)(2,1)}, bf16[128,512]{0,1:T(8,128)(2,1)}, ...) | async-done | bytes 786448 | tf_op jit(solution)/shard_map/psum | solution.py:396
  710.4 1.9 copy.162
  (196 shorter events, 57.0 us)
Async XLA Ops:
  7.2 49.6 %all-gather.5.cloned.1.call-start = ((), (), s32[]{:S(2)}) async-start(), calls=%async_computation.8 | async-start | bytes 7372800 | tf_op jit(solution)/shard_map/all_gather | solution.py:23
  9.6 50.9 %copy-start = (bf16[1,160,1024]{2,1,0:T(8,128)(2,1)S(1)}, bf16[1,160,1024]{2,1,0:T(8,128)(2,1)}, u32[]{:S(2)}) copy-start(bf16[1,160,1024]{2,1,0:T(8,128)(2,1)} %param.14) | copy-start | bytes 983044
  12.1 78.3 %all-gather.7.cloned.1.call-start = ((), (), s32[]{:S(2)}) async-start(), calls=%async_computation.9 | async-start | bytes 2949120 | tf_op jit(solution)/shard_map/all_gather | solution.py:36
  14.7 69.7 %copy-start.13 = (f32[160,64]{0,1:T(8,128)}, f32[160,64]{0,1:T(8,128)S(1)}, u32[]{:S(2)}) copy-start(f32[160,64]{0,1:T(8,128)S(1)} %get-tuple-element.114) | copy-start | bytes 122884
  16.4 65.5 %copy-start.32 = (f32[160]{0:T(256)}, f32[160]{0:T(256)S(1)}, u32[]{:S(2)}) copy-start(f32[160]{0:T(256)S(1)} %get-tuple-element.116) | copy-start | bytes 1924
  60.5 21.4 %copy-start.29 = (f32[1024]{0:T(1024)}, f32[1024]{0:T(1024)S(1)}, u32[]{:S(2)}) copy-start(f32[1024]{0:T(1024)S(1)} %get-tuple-element.73) | copy-start | bytes 12292
  60.5 3.6 copy-start.27
  60.5 3.6 copy-start.28
  61.1 3.9 copy-start.31
  64.0 135.7 %all-gather.9.cloned.1.call-start = ((), (), s32[]{:S(2)}) async-start(), calls=%async_computation.10 | async-start | bytes 4718592 | tf_op jit(solution)/shard_map/all_gather | solution.py:36
  84.7 9.7 %copy-start.25 = (bf16[160,16,64]{0,2,1:T(8,128)(2,1)}, bf16[160,16,64]{0,2,1:T(8,128)(2,1)S(1)}, u32[]{:S(2)}) copy-start(bf16[160,16,64]{0,2,1:T(8,128)(2,1)S(1)} %fusion.92) | copy-start | bytes 983044
  94.4 11.2 %copy-start.4 = (bf16[1280,512]{0,1:T(8,128)(2,1)}, bf16[1280,512]{0,1:T(8,128)(2,1)S(1)}, u32[]{:S(2)}) copy-start(bf16[1280,512]{0,1:T(8,128)(2,1)S(1)} %copy.137) | copy-start | bytes 3932164
  112.7 3.2 copy-start.17
  115.9 0.9 copy-start.2
  137.4 7.7 %copy-start.21 = (bf16[1,160,1024]{2,1,0:T(8,128)(2,1)S(1)}, bf16[1,160,1024]{2,1,0:T(8,128)(2,1)}, u32[]{:S(2)}) copy-start(bf16[1,160,1024]{2,1,0:T(8,128)(2,1)} %param.15) | copy-start | bytes 983044
  137.4 8.7 %copy-start.6 = (bf16[160,1024]{1,0:T(8,128)(2,1)S(1)}, bf16[160,1024]{1,0:T(8,128)(2,1)}, u32[]{:S(2)}) copy-start(bf16[160,1024]{1,0:T(8,128)(2,1)} %multiply_convert_fusion) | copy-start | bytes 983044
  137.4 57.7 %all-to-all-start = ((bf16[16,2,50,1024]{3,1,2,0:T(2,128)(2,1)}), bf16[16,2,50,1024]{3,1,2,0:T(2,128)(2,1)}, u32[]{:S(2)}, u32[]{:S(2)}) async-start(bf16[16,2,50,1024]{3,1,2,0:T(2,128)(2,1)} %copy.146), calls=%async_computation | async-start | bytes 6553600 | tf_op jit(solution)/shard_map/all_to_all | solution.py:219
  144.5 67.6 %all-gather.11.cloned.1.call-start = ((), (), s32[]{:S(2)}) async-start(), calls=%async_computation.11 | async-start | bytes 2359296 | tf_op jit(solution)/shard_map/all_gather | solution.py:127
  195.0 52.1 %all-to-all-start.2 = ((bf16[16,2,50,1024]{3,1,2,0:T(2,128)(2,1)}), bf16[16,2,50,1024]{3,1,2,0:T(2,128)(2,1)S(1)}, u32[]{:S(2)}, u32[]{:S(2)}) async-start(bf16[16,2,50,1024]{3,1,2,0:T(2,128)(2,1)} %copy.152), calls=%async_computation.2 | async-start | bytes 6553600 | tf_op jit(solution)/shard_map/all_to_all | solution.py:243
  199.8 6.6 copy-start.8
  247.1 9.1 %copy-start.10 = (bf16[16,2,50,1024]{3,1,2,0:T(2,128)(2,1)}, bf16[16,2,50,1024]{3,1,2,0:T(2,128)(2,1)S(1)}, u32[]{:S(2)}) copy-start(bf16[16,2,50,1024]{3,1,2,0:T(2,128)(2,1)S(1)} %all-to-all-done.2) | copy-start | bytes 9830404
  247.1 10.3 %copy-start.35 = (bf16[2,512,1024]{2,1,0:T(8,128)(2,1)S(1)}, bf16[2,512,1024]{2,1,0:T(8,128)(2,1)}, u32[]{:S(2)}) copy-start(bf16[2,512,1024]{2,1,0:T(8,128)(2,1)} %all-gather.11.cloned.1.call-done) | copy-start | bytes 6291460
  256.3 1.2 copy-start.36
  264.7 48.4 %all-to-all-start.1 = ((bf16[16,2,50,1024]{3,1,2,0:T(2,128)(2,1)}), bf16[16,2,50,1024]{3,1,2,0:T(2,128)(2,1)S(1)}, u32[]{:S(2)}, u32[]{:S(2)}) async-start(bf16[16,2,50,1024]{3,1,2,0:T(2,128)(2,1)} %copy.149), calls=%async_computation.1 | async-start | bytes 6553600 | tf_op jit(solution)/shard_map/all_to_all | solution.py:226
  268.7 4.4 copy-start.9
  268.7 4.4 copy-start.15
  313.1 49.4 %all-to-all-start.3 = ((bf16[16,2,50,1024]{3,1,2,0:T(2,128)(2,1)}), bf16[16,2,50,1024]{3,1,2,0:T(2,128)(2,1)}, u32[]{:S(2)}, u32[]{:S(2)}) async-start(bf16[16,2,50,1024]{3,1,2,0:T(2,128)(2,1)} %copy.154), calls=%async_computation.3 | async-start | bytes 6553600 | tf_op jit(solution)/shard_map/all_to_all | solution.py:268
  317.6 160.5 %reduce-scatter.13.cloned.1.call-start = ((), (), s32[]{:S(2)}) async-start(), calls=%async_computation.14 | async-start | bytes 2949120
  375.7 3.7 copy-start.3
  375.7 5.2 copy-start.12
  375.7 5.2 copy-start.22
  384.8 7.5 %copy-start.5 = (bf16[1280,512]{0,1:T(8,128)(2,1)S(1)}, bf16[1280,512]{0,1:T(8,128)(2,1)}, u32[]{:S(2)}) copy-start(bf16[1280,512]{0,1:T(8,128)(2,1)} %copy-done.4) | copy-start | bytes 3932164
  392.4 6.6 copy-start.26
  435.5 117.0 %reduce-scatter.11.cloned.1.call-start = ((), (), s32[]{:S(2)}) async-start(), calls=%async_computation.13 | async-start | bytes 2359296 | tf_op jit(solution)/shard_map/reduce_scatter | solution.py:390
  441.9 138.8 %reduce-scatter.15.cloned.1.call-start = ((), (), s32[]{:S(2)}) async-start(), calls=%async_computation.15 | async-start | bytes 7372800
  442.0 30.9 %copy-start.23 = (f32[160,64]{0,1:T(8,128)S(1)}, f32[160,64]{0,1:T(8,128)}, u32[]{:S(2)}) copy-start(f32[160,64]{0,1:T(8,128)} %get-tuple-element.112) | copy-start | bytes 122884
  472.8 0.8 copy-start.14
  472.8 1.8 copy-start.7
  473.2 1.8 copy-start.1
  473.2 1.8 copy-start.30
  473.2 1.8 copy-start.33
  474.6 1.2 copy-start.18
  480.7 1.0 copy-start.24
  480.7 4.9 copy-start.19
  538.9 1.5 copy-start.16
  538.9 81.7 %reduce-scatter.9.cloned.1.call-start = ((), (), s32[]{:S(2)}) async-start(), calls=%async_computation.12 | async-start | bytes 4718592 | tf_op jit(solution)/shard_map/reduce_scatter | solution.py:46
  540.4 4.7 copy-start.20
  552.4 34.0 %copy-start.11 = (f32[160,1024]{1,0:T(8,128)S(1)}, f32[160,1024]{1,0:T(8,128)}, u32[]{:S(2)}) copy-start(f32[160,1024]{1,0:T(8,128)} %get-tuple-element.124) | copy-start | bytes 1966084
  552.4 34.0 %copy-start.34 = (f32[160]{0:T(256)S(1)}, f32[160]{0:T(256)}, u32[]{:S(2)}) copy-start(f32[160]{0:T(256)} %get-tuple-element.115) | copy-start | bytes 1924
  552.4 158.0 %all-reduce.4.cloned.1.call-start = ((), (), s32[]{:S(2)}) async-start(), calls=%async_computation.16 | async-start | bytes 1572864 | tf_op jit(solution)/shard_map/psum | solution.py:396
Sparse Core Ops, SparseCore 0:
  12.2 44.5 all-gather.4
  64.2 26.2 all-gather.6
  92.7 32.6 all-gather.8
  146.7 25.9 all-gather.10
  435.6 32.7 reduce-scatter.12
  470.6 32.4 reduce-scatter.10
  539.0 41.6 reduce-scatter.14
  583.1 37.4 reduce-scatter.8
  624.8 85.5 all-reduce.3
where the time goes:
time: 731 us; the launch traced here: 724 us
  waiting for transfers between devices  268 us (37%)
  matrix products  169 us (23%)
  local copies, waits for them, and re-layouts  153 us (21%)
  other arithmetic  56.7 us (8%)
  blocking collectives  41.8 us (6%)
  starting transfers between devices  20.9 us (3%)
  between operations  15 us (2%)
    psum x1, waiting for transfers between devices, shards(): lax.psum(sum_query.astype(jnp.bfloat16), 'expert').astype(jnp.float32)  42.3 us
    psum x1, blocking collectives, shards(): lax.psum(sum_gain_a.astype(jnp.bfloat16), 'expert').astype(jnp.float32)  41.8 us
    all_gather x1, waiting for transfers between devices, sent_together(): result = lax.all_gather(both, axis, axis=dim, tiled=True)  40.4 us
    concatenate x1, local copies, waits for them, and re-layouts, side_by_side(): jnp.concatenate([a.reshape(*a.shape[:along], w) for a, w in zip(arrays, w...  36.9 us
    all_to_all x1, waiting for transfers between devices, shards(): lax.all_to_all(grad_outgoing, 'expert', split_axis=0, concat_axis=0, tile...  35 us
    reduce_scatter x1, waiting for transfers between devices, sent_together_3(): lax.psum_scatter(both, axis, scatter_dimension=dim, tiled=True)  33.2 us
    all_to_all x1, waiting for transfers between devices, shards(): lax.all_to_all(produced, 'expert', split_axis=0, concat_axis=0, tiled=True)  32.7 us
    dot_general x1, matrix products, shards(): jnp.einsum('hgqk,qhgd->khd', grad_scores, query_rows, preferred_element_t...  31.8 us
  transfers between devices with their start and end apart: 13, of which 9 were waited for; matrix products, arithmetic and copies ran while one was open for 37% of the time, Pallas kernels for 0%

commit v1 on v0

v1 whole, which is shorter than its diff:
```python
import functools

import jax
import jax.numpy as jnp
from jax import lax
from jax.experimental import pallas as pl
from jax.experimental.pallas import tpu as pltpu
from jax.sharding import PartitionSpec as P

MESH = pl.DeviceIdType.MESH
QUERY_HEADS = 16
KEY_VALUE_HEADS = 8
HEAD_SIZE = 64
TOPK = 8
EXPERTS = 32
ROWS = 160
SLOTS = 64
LANES = 256
WIDTH = 1024
EPS = 1e-06
BASE = 10000.0
BF = jnp.bfloat16
F32 = jnp.float32


class Event:
    def __init__(self, copy, arriving):
        self.copy, self.arriving = copy, arriving

    def arrived(self):
        self.arriving.wait_recv()


class Net:
    def __init__(self, send_sem, recv_sem, local_sem):
        self.send_sem, self.recv_sem, self.local_sem = send_sem, recv_sem, local_sem
        self.sent, self.local, self.kept = [], [], 0
        f, e = lax.axis_index("fsdp"), lax.axis_index("expert")
        self.y, self.c = f // 2, lax.rem(f, 2)
        self.z, self.x = e // 4, lax.rem(e, 4)

    def place(self, axis):
        return {"x": self.x, "y": self.y, "z": self.z}[axis]

    def device(self, axis, d):
        y, c, z, x = self.y, self.c, self.z, self.x
        if axis == "core":
            c = 1 - c
        elif axis == "y":
            y = around(y, d)
        elif axis == "z":
            z = around(z, d)
        elif axis == "x":
            x = around(x, d)
        return (y * 2 + c, z * 4 + x)

    def greet(self, axes, group=False):
        barrier = pltpu.get_barrier_semaphore()
        partners = []
        for axis in axes:
            for d in (1,) if axis == "core" else (1, -1):
                partners.append(self.device(axis, d))
        for partner in partners:
            pl.semaphore_signal(barrier, inc=1, device_id=partner, device_id_type=MESH)
        count = len(partners)
        if group:
            e = self.z * 4 + self.x
            for i in range(1, 16):
                pl.semaphore_signal(
                    barrier,
                    inc=1,
                    device_id=(self.y * 2 + self.c, lax.rem(e + i, 16)),
                    device_id_type=MESH,
                )
            count += 15
        pl.semaphore_wait(barrier, count)

    def send(self, src, dst, device, land):
        k = len(self.sent)
        copy = pltpu.make_async_remote_copy(
            src, dst, self.send_sem.at[k], self.recv_sem.at[k], device_id=device, device_id_type=MESH
        )
        copy.start()
        arriving = pltpu.make_async_remote_copy(
            land, land, self.send_sem.at[k], self.recv_sem.at[k], device_id=device, device_id_type=MESH
        )
        self.sent.append(copy)
        return Event(copy, arriving)

    def keep(self, src, dst):
        copy = pltpu.make_async_copy(src, dst, self.local_sem.at[self.kept])
        copy.start()
        self.local.append(copy)
        self.kept += 1

    def settle(self):
        for copy in self.local:
            copy.wait()
        self.local = []

    def finish(self):
        for copy in self.sent:
            copy.wait_send()
        self.settle()


def around(p, d):
    return lax.rem(p + (d + 4), 4)


def in_turn(steps):
    queue = []
    for n, step in enumerate(steps):
        due = next(step, None)
        if due is not None:
            queue.append((due, n))
    while queue:
        queue.sort()
        _, n = queue.pop(0)
        due = next(steps[n], None)
        if due is not None:
            queue.append((due, n))


def us(count):
    return count * 2 / 50e3


def gather_pack(net, inp, out, view, start, size, total):
    y, c = net.y, net.c
    slot = lambda d, core: around(y, d) * 2 + core
    here = lambda d, half=None: view(out, slot(d, c), half)
    there = lambda d, half=None: view(out, slot(d, 1 - c), half)
    right, left, mate = net.device("y", 1), net.device("y", -1), net.device("core", 0)
    to_right = net.send(inp, here(0), right, here(-1))
    to_left = net.send(inp, here(0), left, here(1))
    over = [net.send(inp, here(0), mate, there(0))]
    net.keep(inp, here(0))
    yield 1 + start + size
    to_right.arrived()
    far0 = net.send(here(-1, 0), here(-1, 0), right, here(2, 0))
    over.append(net.send(here(-1), here(-1), mate, there(-1)))
    to_left.arrived()
    far1 = net.send(here(1, 1), here(1, 1), left, here(2, 1))
    over.append(net.send(here(1), here(1), mate, there(1)))
    yield 2 + total + (start + size) / 2
    far0.arrived()
    over.append(net.send(here(2, 0), here(2, 0), mate, there(2, 0)))
    far1.arrived()
    over.append(net.send(here(2, 1), here(2, 1), mate, there(2, 1)))
    yield 1000
    for event in over:
        event.arrived()


def gather_plane(net, inp, out, view, part, start, u):
    one, two = ("x", "z") if part == 0 else ("z", "x")
    p, q = net.place(one), net.place(two)

    def slot(dp, dq):
        a, b = around(p, dp), around(q, dq)
        return b * 4 + a if part == 0 else a * 4 + b

    at = lambda dp, dq, half=None: view(out, slot(dp, dq), part, half)
    own = view(inp, None, part, None)
    right1, left1 = net.device(one, 1), net.device(one, -1)
    right2, left2 = net.device(two, 1), net.device(two, -1)
    to_right = net.send(own, at(0, 0), right1, at(-1, 0))
    to_left = net.send(own, at(0, 0), left1, at(1, 0))

    def spread(dp):
        src = own if dp == 0 else at(dp, 0)
        return (
            dp,
            net.send(src, at(dp, 0), right2, at(dp, -1)),
            net.send(src, at(dp, 0), left2, at(dp, 1)),
        )

    spreads = [spread(0)]
    net.keep(own, at(0, 0))
    yield start + 1 + u
    to_right.arrived()
    far0 = net.send(at(-1, 0, 0), at(-1, 0, 0), right1, at(2, 0, 0))
    spreads.append(spread(-1))
    to_left.arrived()
    far1 = net.send(at(1, 0, 1), at(1, 0, 1), left1, at(2, 0, 1))
    spreads.append(spread(1))
    yield start + 2 + 2 * u
    last = []

    def relay(item):
        dp, from_left, from_right = item
        from_left.arrived()
        last.append(net.send(at(dp, -1, 0), at(dp, -1, 0), right2, at(dp, 2, 0)))
        from_right.arrived()
        last.append(net.send(at(dp, 1, 1), at(dp, 1, 1), left2, at(dp, 2, 1)))

    relay(spreads[0])
    yield start + 2.5 + 2.5 * u
    far0.arrived()
    far1.arrived()
    spreads.append(spread(2))
    yield start + 3 + 3.5 * u
    relay(spreads[1])
    yield start + 3 + 4.5 * u
    relay(spreads[2])
    yield start + 4 + 6 * u
    relay(spreads[3])
    yield 1000
    for event in last:
        event.arrived()


def plain(ref):
    return ref[...].astype(F32)


class Ring:
    def __init__(self, net, axis, source, own, put, landing, sums):
        self.net, self.source, self.own, self.put = net, source, own, put
        self.landing, self.sums = landing, sums
        self.right, self.left = net.device(axis, 1), net.device(axis, -1)

    def go(self, n, src, device):
        return self.net.send(src, self.landing.at[n], device, self.landing.at[n])

    def far(self):
        self.far_right = self.go(0, self.source(2, 0), self.right)
        self.far_left = self.go(1, self.source(2, 1), self.left)

    def near_right(self):
        self.from_left = self.go(2, self.source(1, 1), self.right)

    def near_left(self):
        self.from_right = self.go(3, self.source(-1, 0), self.left)

    def relay(self):
        self.far_right.arrived()
        self.sums[0] = (plain(self.source(1, 0)) + plain(self.landing.at[0])).astype(BF)
        self.sum_right = self.go(4, self.sums.at[0], self.right)
        self.far_left.arrived()
        self.sums[1] = (plain(self.source(-1, 1)) + plain(self.landing.at[1])).astype(BF)
        self.sum_left = self.go(5, self.sums.at[1], self.left)

    def close(self):
        self.from_right.arrived()
        self.sum_right.arrived()
        self.put(0, self.own(0) + plain(self.landing.at[3]) + plain(self.landing.at[4]))
        self.from_left.arrived()
        self.sum_left.arrived()
        self.put(1, self.own(1) + plain(self.landing.at[2]) + plain(self.landing.at[5]))


def sum_plane(net, part, payload, cols, put, landing, sums, accs):
    one, two = ("z", "x") if part == 0 else ("x", "z")
    p, q = net.place(one), net.place(two)
    columns = pl.ds(part * cols, cols)
    half_rows = payload.shape[1] // 2
    u = us(payload.shape[1] * cols)

    def slot(dp, dq):
        a, b = around(p, dp), around(q, dq)
        return a * 4 + b if part == 0 else b * 4 + a

    rings = []
    for n, dq in enumerate((2, 1, -1, 0)):

        def source(d, half, dq=dq):
            return payload.at[slot(d, dq), pl.ds(half * half_rows, half_rows), columns]

        def own(half, source=source):
            return plain(source(0, half))

        def keep(half, value, n=n):
            accs[n, half] = value.astype(BF)

        rings.append(Ring(net, one, source, own, keep, landing.at[n], sums.at[n]))
    at = {2: 0, 1: 1, -1: 2, 0: 3}
    last = Ring(
        net,
        two,
        lambda d, half: accs.at[at[d], half],
        lambda half: plain(accs.at[3, half]),
        put,
        landing.at[4],
        sums.at[4],
    )
    for ring in rings:
        ring.far()
    for ring in rings:
        ring.near_right()
        ring.near_left()
    for n in range(4):
        yield 2 + 0.5 * (n + 1) * u
        rings[n].relay()
    for n in range(4):
        yield 3 + (4 + 0.5 * (n + 1)) * u
        rings[n].close()
        if n == 0:
            last.far()
        elif n == 1:
            last.near_right()
        elif n == 2:
            last.near_left()
    yield 4 + 6.5 * u
    last.relay()
    yield 6 + 7.5 * u
    last.close()


def sum_pack(net, payload, view, put, start, b, pairs, landing, sums):
    y, c = net.y, net.c
    mate = net.device("core", 0)
    order = (2, 1, -1, 0)
    slot = lambda d, core: around(y, d) * 2 + core
    events = [
        net.send(view(payload, slot(d, 1 - c)), pairs.at[n], mate, pairs.at[n])
        for n, d in enumerate(order)
    ]
    at = {2: 0, 1: 1, -1: 2}
    source = lambda d, half: pairs.at[at[d], half]
    own = lambda half: plain(view(payload, slot(0, c)).at[half]) + plain(pairs.at[3, half])
    ring = Ring(net, "y", source, own, put, landing, sums)

    def both(n):
        events[n].arrived()
        for half in range(2):
            pairs[n, half] = (
                plain(view(payload, slot(order[n], c)).at[half]) + plain(pairs.at[n, half])
            ).astype(BF)

    yield 1 + start / 5
    both(0)
    ring.far()
    yield 1 + start / 5 + b / 10
    both(1)
    ring.near_right()
    both(2)
    ring.near_left()
    yield 2 + start + b * 0.6
    ring.relay()
    yield 3 + start + b * 1.5
    events[3].arrived()
    ring.close()


def sum_all(net, part, whole, out, now, landing1, sums1, accs, landing2, sums2, blocks):
    one, two = ("x", "z") if part == 0 else ("z", "x")
    p, q = net.place(one), net.place(two)
    wide = whole.shape[3] // 4

    def keep(half, value):
        for b in range(4):
            accs[b, half] = value[:, b * wide : (b + 1) * wide].astype(BF)

    def block(half, value):
        blocks[q, half] = value.astype(BF)

    ring = Ring(
        net,
        one,
        lambda d, half: whole.at[around(p, d), half],
        lambda half: plain(whole.at[p, half]),
        keep,
        landing1,
        sums1,
    )
    then = Ring(
        net,
        two,
        lambda d, half: accs.at[around(q, d), half],
        lambda half: plain(accs.at[q, half]),
        block,
        landing2,
        sums2,
    )
    for r in (ring, then):
        r.far()
        r.near_right()
        r.near_left()
        now += 2.5
        yield now
        r.relay()
        now += 2.5
        yield now
        r.close()
    for due in ring_gather(net, two, blocks):
        yield now + due
    now += 5
    for b in range(4):
        for half in range(2):
            out[p, half, :, b * wide : (b + 1) * wide] = blocks[b, half]
    for due in ring_gather(net, one, out):
        yield now + due


def ring_gather(net, axis, ref):
    p = net.place(axis)
    right, left = net.device(axis, 1), net.device(axis, -1)
    at = lambda d: ref.at[around(p, d)]
    to_right = net.send(at(0), at(0), right, at(-1))
    to_left = net.send(at(0), at(0), left, at(1))
    yield 2.5
    to_right.arrived()
    far0 = net.send(at(-1).at[0], at(-1).at[0], right, at(2).at[0])
    to_left.arrived()
    far1 = net.send(at(1).at[1], at(1).at[1], left, at(2).at[1])
    yield 5
    far0.arrived()
    far1.arrived()


def swap_small(net, payload, out):
    e = net.z * 4 + net.x
    f = net.y * 2 + net.c
    events = []
    for i in range(1, 16):
        to, source = lax.rem(e + i, 16), lax.rem(e + (16 - i), 16)
        events.append(net.send(payload.at[to], out.at[e], (f, to), out.at[source]))
    net.keep(payload.at[e], out.at[e])
    yield 1000
    for event in events:
        event.arrived()


ANY = pl.BlockSpec(memory_space=pl.ANY)
INSIDE = pl.BlockSpec(memory_space=pltpu.VMEM)


def call(kernel, ident, ins, outs, in_space, out_space, scratch, events, keeps):
    return pl.pallas_call(
        kernel,
        out_shape=outs,
        in_specs=in_space,
        out_specs=out_space,
        scratch_shapes=[
            *scratch,
            pltpu.SemaphoreType.DMA((events,)),
            pltpu.SemaphoreType.DMA((events,)),
            pltpu.SemaphoreType.DMA((max(keeps, 1),)),
        ],
        compiler_params=pltpu.CompilerParams(
            collective_id=ident, has_side_effects=True, vmem_limit_bytes=56 << 20
        ),
    )(*ins)


def rows_view(ref, slot, half):
    rows = ref.shape[1]
    if half is None:
        return ref.at[slot]
    return ref.at[slot, pl.ds(half * (rows // 2), rows // 2)]


def pair_view(ref, slot, half):
    if half is None:
        return ref.at[:, slot]
    return ref.at[half, slot]


def plane_view(ref, slot, part, half):
    rows, cols = ref.shape[-2] // 2, ref.shape[-1] // 2
    where = () if slot is None else (slot,)
    if half is None:
        return ref.at[(*where, slice(None), pl.ds(part * cols, cols))]
    return ref.at[(*where, pl.ds(half * rows, rows), pl.ds(part * cols, cols))]


def quarter_view(ref, slot, part, half):
    where = () if slot is None else (slot,)
    if half is None:
        return ref.at[(*where, pl.ds(part * 2, 2))]
    return ref.at[(*where, part * 2 + half)]


def gather_kernel(views, planes, *refs):
    packs = len(views)
    total = packs + planes
    ins, outs = refs[:total], refs[total : 2 * total]
    net = Net(*refs[2 * total :])
    net.greet((["core", "y"] if packs else []) + (["x", "z"] if planes else []))
    steps, start = [], 0.0
    for i in range(planes):
        inp, out = ins[packs + i], outs[packs + i]
        u = us(inp.shape[0] * inp.shape[1] // 2)
        for part in range(2):
            steps.append(gather_plane(net, inp, out, plane_view, part, start, u))
        start += u / 2
    sizes = [us(functools.reduce(lambda a, b: a * b, r.shape)) for r in ins[:packs]]
    start = 0.0
    for i in range(packs):
        steps.append(gather_pack(net, ins[i], outs[i], views[i], start, sizes[i], sum(sizes)))
        start += sizes[i]
    in_turn(steps)
    net.finish()


def gather(ident, pack_arrays, plane_arrays):
    views, outs = [], []
    for a in pack_arrays:
        if a.ndim == 2:
            views.append(rows_view)
            outs.append(jax.ShapeDtypeStruct((8, *a.shape), a.dtype))
        else:
            views.append(pair_view)
            outs.append(jax.ShapeDtypeStruct((a.shape[0], 8, *a.shape[1:]), a.dtype))
    for a in plane_arrays:
        outs.append(jax.ShapeDtypeStruct((16, *a.shape), a.dtype))
    n, m = len(pack_arrays), len(plane_arrays)
    result = call(
        functools.partial(gather_kernel, tuple(views), m),
        ident,
        [*pack_arrays, *plane_arrays],
        outs,
        [ANY] * (n + m),
        [ANY] * (n + m),
        [],
        9 * n + 40 * m,
        n + 2 * m,
    )
    packed = []
    for a, r in zip(pack_arrays, result[:n]):
        if a.ndim == 2:
            packed.append(r.reshape(8 * a.shape[0], a.shape[1]))
        else:
            packed.append(r.reshape(a.shape[0], 8 * a.shape[1], a.shape[2]))
    return packed, result[n:]


def put_into(ref):
    def put(half, value):
        ref[half] = value.astype(ref.dtype)

    return put


def block_view(ref, slot):
    return ref.at[slot]


def pair_block_view(ref, slot):
    return ref.at[:, slot]


def scatter_kernel(kinds, planes, swaps, finals, *refs):
    refs = list(refs)
    take = lambda n: [refs.pop(0) for _ in range(n)]
    packs = len(kinds)
    pack_in, plane_in, swap_in = take(packs), take(planes), take(swaps)
    pack_out, plane_out, swap_out = take(packs), take(planes), take(swaps)
    pack_scratch = [take(3) for _ in range(packs)]
    plane_scratch = [[take(3) for _ in range(2)] for _ in range(planes)]
    small = [finals and r.shape[-1] == 128 for r in pack_in]
    final_scratch = [take(2 if small[i] else 7) for i in range(packs)] if finals else []
    net = Net(*refs)
    wide = planes or swaps or finals
    net.greet((["core", "y"] if packs else []) + (["x", "z"] if wide else []), group=bool(swaps))
    steps = []
    for i in range(planes):
        for part in range(2):
            cols = WIDTH // 2

            def put(half, value, i=i, part=part, cols=cols):
                rows = plane_in[i].shape[1] // 2
                plane_out[i][
                    half * rows : (half + 1) * rows, part * cols : (part + 1) * cols
                ] = value.astype(plane_out[i].dtype)

            steps.append(sum_plane(net, part, plane_in[i], cols, put, *plane_scratch[i][part]))
    for i in range(swaps):
        steps.append(swap_small(net, swap_in[i], swap_out[i]))

    def dense(i, start, b):
        whole, rest = final_scratch[i][0], final_scratch[i][1:]

        def put(half, value):
            n = value.shape[-1]
            whole[half * 2 : half * 2 + 2] = value.reshape(2, 2, 16, n).astype(BF)

        yield from sum_pack(net, pack_in[i], kinds[i], put, start, b, *pack_scratch[i])
        yield from sum_all(net, i % 2, whole, pack_out[i], start + 1.5 * b + 3, *rest)

    def narrow(i, start, b):
        whole, landed = final_scratch[i]

        def put(half, value):
            whole[half * 2 : half * 2 + 2] = value.reshape(2, 32, 128).astype(BF)

        yield from sum_pack(net, pack_in[i], kinds[i], put, start, b, *pack_scratch[i])
        now = start + 1.5 * b + 3
        parts = [
            gather_plane(net, whole, landed, quarter_view, part, now, 1.0) for part in range(2)
        ]
        while parts:
            due = [next(p, None) for p in parts]
            if None in due:
                break
            yield max(due)
        net.settle()
        total = plain(landed.at[0])
        for n in range(1, 16):
            total = total + plain(landed.at[n])
        pack_out[i][...] = total

    start = 0.0
    for i in range(packs):
        values = functools.reduce(lambda a, b: a * b, pack_in[i].shape) // 8
        b = us(values)
        scratch = pack_scratch[i]
        if not finals:
            put = put_into(pack_out[i])
            steps.append(sum_pack(net, pack_in[i], kinds[i], put, start, b, *scratch))
        elif small[i]:
            steps.append(narrow(i, start, b))
        else:
            steps.append(dense(i, start, b))
        start += 1.5 * b
    in_turn(steps)
    net.finish()


def scatter(ident, pack_arrays, plane_arrays, swap_arrays=(), finals=False):
    kinds, outs, scratch, keeps = [], [], [], len(swap_arrays)
    for a in pack_arrays:
        if a.shape[0] == 2:
            kinds.append(pair_block_view)
            block = (2, *a.shape[2:])
        else:
            kinds.append(block_view)
            block = a.shape[1:]
        half = block[1:]
        if finals and block[-1] == 128:
            outs.append(jax.ShapeDtypeStruct((4, 32, 128), F32))
        elif finals:
            outs.append(jax.ShapeDtypeStruct((4, 2, 16, block[-1]), BF))
        else:
            outs.append(jax.ShapeDtypeStruct(block, BF))
        scratch += [
            pltpu.VMEM((4, *block), BF),
            pltpu.VMEM((6, *half), BF),
            pltpu.VMEM((2, *half), BF),
        ]
    for a in plane_arrays:
        rows, cols = a.shape[1] // 2, a.shape[2] // 2
        outs.append(jax.ShapeDtypeStruct(a.shape[1:], F32))
        for _ in range(2):
            scratch += [
                pltpu.VMEM((5, 6, rows, cols), BF),
                pltpu.VMEM((5, 2, rows, cols), BF),
                pltpu.VMEM((4, 2, rows, cols), BF),
            ]
    for a in swap_arrays:
        outs.append(jax.ShapeDtypeStruct(a.shape, a.dtype))
    events = 10 * len(pack_arrays) + 60 * len(plane_arrays) + 15 * len(swap_arrays)
    if finals:
        for a in pack_arrays:
            n = a.shape[-1]
            if n == 128:
                scratch += [pltpu.VMEM((4, 32, 128), BF), pltpu.VMEM((16, 4, 32, 128), BF)]
                events += 40
                keeps += 2
                continue
            scratch += [
                pltpu.VMEM((4, 2, 16, n), BF),
                pltpu.VMEM((6, 16, n), BF),
                pltpu.VMEM((2, 16, n), BF),
                pltpu.VMEM((4, 2, 16, n // 4), BF),
                pltpu.VMEM((6, 16, n // 4), BF),
                pltpu.VMEM((2, 16, n // 4), BF),
                pltpu.VMEM((4, 2, 16, n // 4), BF),
            ]
            events += 20
    ins = [*pack_arrays, *plane_arrays, *swap_arrays]
    return call(
        functools.partial(
            scatter_kernel, tuple(kinds), len(plane_arrays), len(swap_arrays), finals
        ),
        ident,
        ins,
        outs,
        [INSIDE] * len(ins),
        [INSIDE] * len(ins),
        scratch,
        events,
        keeps,
    )


KEYS = 8 * ROWS
BLOCK = 256
FOUR = 4 * ROWS


def dot_last(a, b):
    return lax.dot_general(a, b, (((1,), (1,)), ((), ())), preferred_element_type=F32)


def dot_first(a, b):
    return lax.dot_general(a, b, (((0,), (0,)), ((), ())), preferred_element_type=F32)


def low_lanes(rows):
    return lax.broadcasted_iota(jnp.int32, (rows, 128), 1) < HEAD_SIZE


def four_heads(v):
    low = low_lanes(ROWS)
    a, b = v[:, :128], v[:, 128:]
    zero = jnp.zeros_like(a)
    return jnp.concatenate(
        [
            jnp.where(low, a, zero),
            jnp.where(low, pltpu.roll(a, HEAD_SIZE, 1), zero),
            jnp.where(low, zero, pltpu.roll(b, HEAD_SIZE, 1)),
            jnp.where(low, zero, b),
        ],
        axis=0,
    )


def side_by_side(v):
    low = low_lanes(ROWS)
    r = [v[i * ROWS : (i + 1) * ROWS] for i in range(4)]
    return jnp.concatenate(
        [
            jnp.where(low, r[0], pltpu.roll(r[1], HEAD_SIZE, 1)),
            jnp.where(low, pltpu.roll(r[2], HEAD_SIZE, 1), r[3]),
        ],
        axis=1,
    )


def set_bias(span_ref, bias):
    @pl.when(pl.program_id(0) == 0)
    def _():
        first, last = span_ref[0:1, :], span_ref[1:2, :]
        for b in range(0, KEYS, BLOCK):
            at = lax.broadcasted_iota(jnp.int32, (BLOCK, FOUR), 0) + b
            bias[b : b + BLOCK] = jnp.where((at >= first) & (at <= last), 0.0, -1e30)


def attend_kernel(q_ref, k_ref, v_ref, span_ref, o_ref, lse_ref, bias, score):
    set_bias(span_ref, bias)
    q = four_heads(q_ref[...].astype(F32) * HEAD_SIZE ** (-0.5)).astype(BF)
    top = jnp.full((1, FOUR), -3e38, F32)
    for b in range(0, KEYS, BLOCK):
        s = dot_last(k_ref[b : b + BLOCK], q) + bias[b : b + BLOCK]
        score[b : b + BLOCK] = s
        top = jnp.maximum(top, jnp.max(s, axis=0, keepdims=True))
    total = jnp.zeros((1, FOUR), F32)
    out = jnp.zeros((128, FOUR), F32)
    for b in range(0, KEYS, BLOCK):
        e = jnp.exp(score[b : b + BLOCK] - top)
        total = total + jnp.sum(e, axis=0, keepdims=True)
        out = out + dot_first(v_ref[b : b + BLOCK], e.astype(BF))
    o_ref[...] = side_by_side((out / total).T).astype(BF)
    lse_ref[0] = jnp.broadcast_to(top + jnp.log(total), (8, FOUR))


def attend(query, kv, span):
    return pl.pallas_call(
        attend_kernel,
        grid=(4,),
        in_specs=[
            pl.BlockSpec((ROWS, 256), lambda p: (0, p)),
            pl.BlockSpec((KEYS, 128), lambda p: (0, p)),
            pl.BlockSpec((KEYS, 128), lambda p: (0, 4 + p)),
            pl.BlockSpec((8, FOUR), lambda p: (0, 0)),
        ],
        out_specs=[
            pl.BlockSpec((ROWS, 256), lambda p: (0, p)),
            pl.BlockSpec((1, 8, FOUR), lambda p: (p, 0, 0)),
        ],
        out_shape=[
            jax.ShapeDtypeStruct((ROWS, WIDTH), BF),
            jax.ShapeDtypeStruct((4, 8, FOUR), F32),
        ],
        scratch_shapes=[pltpu.VMEM((KEYS, FOUR), F32), pltpu.VMEM((KEYS, FOUR), F32)],
        compiler_params=pltpu.CompilerParams(vmem_limit_bytes=48 << 20),
    )(query, kv, kv, span)


def attend_back_kernel(
    q_ref, k_ref, v_ref, g_ref, o_ref, lse_ref, span_ref, dq_ref, dk_ref, dv_ref, bias
):
    set_bias(span_ref, bias)
    q = four_heads(q_ref[...].astype(F32) * HEAD_SIZE ** (-0.5)).astype(BF)
    wide = four_heads(g_ref[...].astype(F32))
    g = wide.astype(BF)
    spread = jnp.sum((wide * four_heads(o_ref[...].astype(F32))).T, axis=0, keepdims=True)
    lse = lse_ref[0, 0:1, :]
    dq = jnp.zeros((128, FOUR), F32)
    for b in range(0, KEYS, BLOCK):
        k = k_ref[b : b + BLOCK]
        p = jnp.exp(dot_last(k, q) + bias[b : b + BLOCK] - lse)
        dp = dot_last(v_ref[b : b + BLOCK], g)
        ds = (p * (dp - spread)).astype(BF)
        dv_ref[b : b + BLOCK] = jnp.dot(p.astype(BF), g, preferred_element_type=F32).astype(BF)
        dk_ref[b : b + BLOCK] = jnp.dot(ds, q, preferred_element_type=F32).astype(BF)
        dq = dq + dot_first(k, ds)
    dq_ref[...] = side_by_side(dq.T * HEAD_SIZE ** (-0.5))


def attend_back(query, kv, grad, attended, lse, span):
    return pl.pallas_call(
        attend_back_kernel,
        grid=(4,),
        in_specs=[
            pl.BlockSpec((ROWS, 256), lambda p: (0, p)),
            pl.BlockSpec((KEYS, 128), lambda p: (0, p)),
            pl.BlockSpec((KEYS, 128), lambda p: (0, 4 + p)),
            pl.BlockSpec((ROWS, 256), lambda p: (0, p)),
            pl.BlockSpec((ROWS, 256), lambda p: (0, p)),
            pl.BlockSpec((1, 8, FOUR), lambda p: (p, 0, 0)),
            pl.BlockSpec((8, FOUR), lambda p: (0, 0)),
        ],
        out_specs=[
            pl.BlockSpec((ROWS, 256), lambda p: (0, p)),
            pl.BlockSpec((KEYS, 128), lambda p: (0, p)),
            pl.BlockSpec((KEYS, 128), lambda p: (0, p)),
        ],
        out_shape=[
            jax.ShapeDtypeStruct((ROWS, WIDTH), F32),
            jax.ShapeDtypeStruct((KEYS, 512), BF),
            jax.ShapeDtypeStruct((KEYS, 512), BF),
        ],
        scratch_shapes=[pltpu.VMEM((KEYS, FOUR), F32)],
        compiler_params=pltpu.CompilerParams(vmem_limit_bytes=48 << 20),
    )(query, kv, kv, grad, attended, lse, span)


def contract_first(left_op, right_op):
    return lax.dot_general(left_op, right_op, (((0,), (0,)), ((), ())), preferred_element_type=F32)


def contract_last(left_op, right_op):
    return lax.dot_general(left_op, right_op, (((1,), (1,)), ((), ())), preferred_element_type=F32)


def rotary(offset, width):
    half_dim = HEAD_SIZE // 2
    lane = jnp.arange(width, dtype=jnp.int32)
    frequency = BASE ** (-2.0 * (lane % half_dim).astype(F32) / HEAD_SIZE)
    angles = offset.astype(F32)[:, None] * frequency[None, :]
    return jnp.cos(angles), jnp.sin(angles)


def swapped(v):
    half_dim = HEAD_SIZE // 2
    first = (jnp.arange(v.shape[1], dtype=jnp.int32) % HEAD_SIZE < half_dim)[None, :]
    return jnp.where(first, -jnp.roll(v, -half_dim, axis=1), jnp.roll(v, half_dim, axis=1))


def norm_back(inputs, inverse_rms, gain_vec, upstream):
    scaled = upstream * gain_vec
    gain_grad = jnp.sum(upstream * inputs * inverse_rms, axis=0)
    spread = jnp.mean(scaled * inputs, axis=-1, keepdims=True)
    return (inverse_rms * scaled - inputs * inverse_rms**3 * spread, gain_grad)


def mm(pattern, a, b):
    return jnp.einsum(pattern, a, b, preferred_element_type=F32)


def shards(
    hidden_in,
    grad_out,
    lengths,
    experts,
    gain_attn,
    w_query,
    key_weight,
    value_weight,
    w_out,
    gain_moe,
    w_router,
    expert_gate,
    expert_up,
    expert_down,
):
    fsdp = lax.axis_index("fsdp")
    owner = lax.axis_index("expert")
    inputs = hidden_in[0].astype(F32)
    upstream = grad_out[0].astype(F32)
    picked = experts[0]

    named = jnp.any(
        picked[None, :, :] == jnp.arange(EXPERTS, dtype=jnp.int32)[:, None, None], axis=-1
    )
    named_wide = jnp.pad(named.astype(BF), ((0, 0), (0, LANES - ROWS)))
    small = jnp.concatenate(
        [w_router, gain_attn[:, None], gain_moe[:, None], jnp.zeros((128, 94), BF)], axis=1
    )
    (full_query, full_key, full_value, full_out, full_small), (all_up, all_named) = gather(
        0, [w_query, key_weight, value_weight, w_out, small], [grad_out[0], named_wide]
    )
    full_router = full_small[:, :EXPERTS]
    full_gain_a = full_small[:, EXPERTS].astype(F32)
    full_gain_m = full_small[:, EXPERTS + 1].astype(F32)

    seq_lengths = lengths[0]
    seq_ends = jnp.cumsum(seq_lengths, dtype=jnp.int32)
    starts = seq_ends - seq_lengths

    def places(index):
        inside = (index[:, None] >= starts[None, :]) & (index[:, None] < seq_ends[None, :])
        inside = inside.astype(jnp.int32)
        return jnp.sum(inside * (index[:, None] - starts[None, :]), axis=1)

    own_index = fsdp * ROWS + jnp.arange(ROWS, dtype=jnp.int32)
    own_offset = places(own_index)
    cosine, sine = rotary(own_offset, WIDTH)
    cosine_k, sine_k = cosine[:, :512], sine[:, :512]
    span = jnp.concatenate(
        [
            jnp.tile(own_index - own_offset, 4)[None, :],
            jnp.tile(own_index, 4)[None, :],
            jnp.zeros((6, FOUR), jnp.int32),
        ]
    )

    inverse_a = lax.rsqrt(jnp.mean(inputs * inputs, axis=-1, keepdims=True) + EPS)
    normed = (inputs * inverse_a * full_gain_a).astype(BF)
    query = jnp.dot(normed, full_query, preferred_element_type=F32)
    key = jnp.dot(normed, full_key, preferred_element_type=F32)
    value = jnp.dot(normed, full_value, preferred_element_type=F32).astype(BF)
    query = (query * cosine + swapped(query) * sine).astype(BF)
    key = (key * cosine_k + swapped(key) * sine_k).astype(BF)
    (kv,), _ = gather(1, [jnp.concatenate([key, value], axis=1)], [])
    attended, lse = attend(query, kv, span)
    hidden = inputs + jnp.dot(attended, full_out, preferred_element_type=F32)
    inverse_m = lax.rsqrt(jnp.mean(hidden * hidden, axis=-1, keepdims=True) + EPS)
    routed = (hidden * inverse_m * full_gain_m).astype(BF)

    (full_gate, full_up, full_down), (all_routed,) = gather(
        2, [expert_gate, expert_up, expert_down], [routed]
    )
    all_named = all_named[:, :, :ROWS]
    logits = mm("de,std->set", full_router, all_routed)
    logits = jnp.where(all_named > 0, logits, -1e30)
    own_logits = lax.dynamic_slice_in_dim(logits, 2 * owner, 2, axis=1)
    own_named = lax.dynamic_slice_in_dim(all_named, 2 * owner, 2, axis=1)
    top = jnp.max(logits, axis=1, keepdims=True)
    total = jnp.sum(jnp.exp(logits - top), axis=1, keepdims=True)
    own_gates = jnp.exp(own_logits - top) / total * own_named.astype(F32)
    before = (
        jnp.arange(ROWS, dtype=jnp.int32)[:, None] < jnp.arange(ROWS, dtype=jnp.int32)[None, :]
    ).astype(BF)
    rank = mm("sjt,tu->sju", own_named, before).astype(jnp.int32)
    pick = (
        (rank[:, :, None, :] == jnp.arange(SLOTS, dtype=jnp.int32)[None, None, :, None])
        & (own_named[:, :, None, :] > 0)
    ).astype(BF)
    slot_gates = jnp.sum(pick.astype(F32) * own_gates[:, :, None, :], axis=-1)
    taken = mm("sjct,std->jscd", pick, all_routed).astype(BF).reshape(2, 16 * SLOTS, WIDTH)
    taken_up = mm("sjct,std->jscd", pick, all_up).astype(BF).reshape(2, 16 * SLOTS, WIDTH)
    slot_gates = slot_gates.transpose(1, 0, 2).reshape(2, 16 * SLOTS, 1)
    gate_part = mm("jrd,jdf->jrf", taken, full_gate)
    up_part = mm("jrd,jdf->jrf", taken, full_up)
    sigmoid_gate = jax.nn.sigmoid(gate_part)
    inner = (gate_part * sigmoid_gate * up_part).astype(BF)
    produced = mm("jrf,jfd->jrd", inner, full_down).astype(BF).astype(F32)
    up_rows = taken_up.astype(F32)
    gate_dots = jnp.sum(produced * up_rows, axis=-1).reshape(2, 16, SLOTS)
    weighed = (slot_gates * produced).astype(BF).reshape(2, 16, SLOTS, WIDTH)
    grad_rows = (slot_gates * up_rows).astype(BF)
    part_out = mm("sjct,jscd->std", pick, weighed).astype(BF)
    grad_inner = mm("jrd,jfd->jrf", grad_rows, full_down)
    grad_gate_part = (
        grad_inner * up_part * sigmoid_gate * (1.0 + gate_part * (1.0 - sigmoid_gate))
    ).astype(BF)
    grad_up_part = (grad_inner * gate_part * sigmoid_gate).astype(BF)
    grad_taken = (
        mm("jrf,jdf->jrd", grad_gate_part, full_gate) + mm("jrf,jdf->jrd", grad_up_part, full_up)
    ).astype(BF)
    part_grad = mm("sjct,jscd->std", pick, grad_taken.reshape(2, 16, SLOTS, WIDTH)).astype(BF)
    grad_down_w = mm("jrf,jrd->jfd", inner, grad_rows).astype(BF)
    grad_gate_w = mm("jrd,jrf->jdf", taken, grad_gate_part).astype(BF)
    grad_up_w = mm("jrd,jrf->jdf", taken, grad_up_part).astype(BF)
    token_dots = jnp.sum(pick.astype(F32) * gate_dots.transpose(1, 0, 2)[:, :, :, None], axis=2)
    token_dots = jnp.pad(token_dots, ((0, 0), (0, 6), (0, LANES - ROWS)))
    sum_gate, sum_up, sum_down, grad_routed, dots = scatter(
        3,
        [
            grad_gate_w.reshape(2, 8, 128, 512),
            grad_up_w.reshape(2, 8, 128, 512),
            grad_down_w.reshape(2, 8, 64, 1024),
        ],
        [part_grad],
        [token_dots],
    )

    dots = dots[:, :2, :ROWS].reshape(EXPERTS, ROWS)
    here = jnp.where(named, contract_last(full_router.T, routed), -1e30)
    here = jnp.exp(here - jnp.max(here, axis=0, keepdims=True)) * named.astype(F32)
    gates = here / jnp.sum(here, axis=0, keepdims=True)
    grad_logits = (gates * (dots - jnp.sum(gates * dots, axis=0, keepdims=True))).astype(BF)
    grad_routed = grad_routed + mm("et,de->td", grad_logits, full_router)
    grad_router_w = mm("td,et->de", routed, grad_logits)
    grad_middle, grad_gain_m = norm_back(hidden, inverse_m, full_gain_m, grad_routed)
    grad_hidden = upstream + grad_middle
    grad_hidden_low = grad_hidden.astype(BF)
    grad_out_w = contract_first(attended, grad_hidden_low)
    grad_attended = contract_last(grad_hidden_low, full_out).astype(BF)
    grad_query, grad_key, grad_value = attend_back(query, kv, grad_attended, attended, lse, span)
    grad_key, grad_value = scatter(
        4, [grad_key.reshape(8, 2, 80, 512), grad_value.reshape(8, 2, 80, 512)], []
    )
    grad_key = grad_key.reshape(ROWS, 512).astype(F32)
    grad_value = grad_value.reshape(ROWS, 512)
    grad_query = (grad_query * cosine - swapped(grad_query) * sine).astype(BF)
    grad_key = (grad_key * cosine_k - swapped(grad_key) * sine_k).astype(BF)
    grad_kv = jnp.concatenate([grad_key, grad_value], axis=1)
    grad_query_w = contract_first(normed, grad_query).astype(BF)
    grad_kv_w = contract_first(normed, grad_kv).astype(BF)
    grad_normed = (
        contract_last(grad_query, full_query)
        + contract_last(grad_key, full_key)
        + contract_last(grad_value, full_value)
    )
    grad_first, grad_gain_a = norm_back(inputs, inverse_a, full_gain_a, grad_normed)
    grad_input = (grad_hidden + grad_first).astype(BF)
    grad_small = jnp.concatenate(
        [
            grad_router_w.astype(BF),
            grad_gain_a.astype(BF)[:, None],
            grad_gain_m.astype(BF)[:, None],
            jnp.zeros((WIDTH, 128 - 34), BF),
        ],
        axis=1,
    )
    block = lambda a: a.reshape(8, 2, 64, a.shape[-1])
    tot_query, tot_out, tot_kv, tot_small, moe_out = scatter(
        5,
        [block(grad_query_w), block(grad_out_w.astype(BF)), block(grad_kv_w), block(grad_small)],
        [part_out],
        finals=True,
    )
    output = (hidden + moe_out).astype(BF)
    flat = lambda a: a.reshape(128, a.shape[-1]).astype(F32)
    tot_kv, tot_small = flat(tot_kv), flat(tot_small)
    return (
        output[None],
        grad_input[None],
        tot_small[:, EXPERTS],
        flat(tot_query),
        tot_kv[:, :512],
        tot_kv[:, 512:],
        flat(tot_out),
        tot_small[:, EXPERTS + 1],
        tot_small[:, :EXPERTS],
        sum_gate.astype(F32),
        sum_up.astype(F32),
        sum_down.astype(F32),
    )


def solution(mesh):
    token, matrix, stack = P("expert", "fsdp", None), P("fsdp", None), P("expert", "fsdp", None)
    return jax.shard_map(
        shards,
        mesh=mesh,
        in_specs=(
            token,
            token,
            P("expert", None),
            token,
            P("fsdp"),
            matrix,
            matrix,
            matrix,
            matrix,
            P("fsdp"),
            matrix,
            stack,
            stack,
            stack,
        ),
        out_specs=(
            token,
            token,
            P("fsdp"),
            matrix,
            matrix,
            matrix,
            matrix,
            P("fsdp"),
            matrix,
            stack,
            stack,
            stack,
        ),
        check_vma=False,
    )
```

time: 731 us -> 409 us (0.56)
  Pallas kernels: 0 us -> 272 us
  waiting for transfers between devices: 268 us -> 0 us
  local copies, waits for them, and re-layouts: 153 us -> 15.9 us
  matrix products: 169 us -> 77.9 us
  blocking collectives: 41.8 us -> 0 us
  other arithmetic: 56.7 us -> 35.6 us
  starting transfers between devices: 20.9 us -> 0 us
  between operations: 15 us -> 1.58 us
    pallas_call x0 -> x8, Pallas kernels: none -> 272 us  [the longest x6 251 us: call(): pl.pallas_call(kernel, out_shape=outs, in_specs=in_space, out_specs=out_s...]
    all_to_all x4 -> x0, waiting for transfers between devices: 119 us -> none  [the longest x1 35 us: shards(): lax.all_to_all(grad_outgoing, 'expert', split_axis=0, concat_axis=0, tile...]
    dot_general x19 -> x21, matrix products: 139 us -> 64.4 us  [the longest x17 59 us: mm(): return jnp.einsum(pattern, a, b, preferred_element_type=F32)]
    all_gather x4 -> x0, waiting for transfers between devices: 46.1 us -> none  [the longest x1 40.4 us: sent_together(): result = lax.all_gather(both, axis, axis=dim, tiled=True)]
    psum x1 -> x0, waiting for transfers between devices: 42.3 us -> none  [shards(): lax.psum(sum_query.astype(jnp.bfloat16), 'expert').astype(jnp.float32)]
    psum x1 -> x0, blocking collectives: 41.8 us -> none  [shards(): lax.psum(sum_gain_a.astype(jnp.bfloat16), 'expert').astype(jnp.float32)]
    concatenate x2, local copies, waits for them, and re-layouts: 39.4 us -> 0.15 us  [the longest x1 0.08 us: shards(): jnp.concatenate([jnp.tile(own_index - own_offset, 4)[None, :], jnp.tile(o...]
    reduce_scatter x2 -> x0, waiting for transfers between devices: 33.2 us -> none  [the longest x1 33.2 us: sent_together_3(): lax.psum_scatter(both, axis, scatter_dimension=dim, tiled=True)]
  transfers between devices with their start and end apart: 13 -> 0, of which waited for: 9 -> 0; matrix products, arithmetic and copies ran while one was open for 37% -> 0% of each run, Pallas kernels for 0% -> 0%
where the time goes in v1:
time: 409 us; the launch traced here: 403 us
  Pallas kernels  272 us (67%)
  matrix products  77.9 us (19%)
  other arithmetic  35.6 us (9%)
  local copies, waits for them, and re-layouts  15.9 us (4%)
    pallas_call x6, Pallas kernels, call(): pl.pallas_call(kernel, out_shape=outs, in_specs=in_space, out_specs=out_s...  251 us
    dot_general x17, matrix products, mm(): return jnp.einsum(pattern, a, b, preferred_element_type=F32)  59 us
    pallas_call x1, Pallas kernels, attend_back(): pl.pallas_call(attend_back_kernel, grid=(4,), in_specs=[pl.BlockSpec((ROW...  12 us
    pallas_call x1, Pallas kernels, attend(): pl.pallas_call(attend_kernel, grid=(4,), in_specs=[pl.BlockSpec((ROWS, 25...  8.68 us

profile of v1, /device:TPU:0, one launch (start us, length us, event | category | flops | bytes accessed | tf_op | source)
XLA Modules:
  0.0 402.5 jit_solution(1659923118685365421)
XLA Ops:
  0.7 0.8 reduce-window.4
  2.3 0.8 copy.114
  3.0 0.8 copy.113
  3.8 0.8 copy.112
  4.7 0.7 maximum_maximum_fusion.1.refs_4_
  5.4 0.8 fusion.76
  6.8 43.3 %shard_map.229 = (bf16[8,128,1024]{2,1,0:T(8,128)(2,1)}, bf16[8,128,512]{2,1,0:T(8,128)(2,1)}, bf16[8,128,512]{2,1,0:T(8,128)(2,1)}, bf16[8,128,1024]{2,1,0:T(8,...) custom-call(bf16[128,1024]{1,0:T(8,128)(2,1)} %refs_0_.2, ...), custom_call_target="tpu_custom_call" | custom-call | tf_op jit(solution)/shard_map/pallas_call | solution.py:431
  50.1 2.0 slice_convert_fusion
  52.3 1.1 fusion.41
  53.5 2.4 fusion.109
  56.2 2.9 multiply_cosine_fusion
  60.4 0.8 pad_maximum_fusion.refs_0_
  61.2 17.4 %shard_map.230 = bf16[8,160,1024]{2,1,0:T(8,128)(2,1)} custom-call(bf16[160,1024]{1,0:T(8,128)(2,1)} %pad_maximum_fusion.refs_0_), custom_call_target="tpu_custom_call" | custom-call | tf_op jit(solution)/shard_map/pallas_call | solution.py:431
  78.9 1.7 copy-done
  80.7 8.7 %shard_map.231 = (bf16[160,1024]{1,0:T(8,128)(2,1)S(1)}, f32[4,8,640]{2,1,0:T(8,128)S(1)}) custom-call(bf16[160,1024]{1,0:T(8,128)(2,1)S(1)} %get-tuple-element.104.q_ref, bf16[1280,1024]{1,0:T(8,128)(2,1)S(1)} %bitcast.186, bf16[1280,1024]{1,0:T(8,128)(2,1)S(1)} %bitcast.187, s32[8,640]{1,0:T(8,128)S(1)} %add_add_fusion.span_ref), custom_call_target="tpu_custom_call" | custom-call | tf_op jit(solution)/shard_map/pallas_call | solution.py:761
  89.4 2.3 multiply_reduce_fusion.2
  91.8 0.9 multiply_convert_fusion.3.refs_3_
  92.7 38.9 %shard_map.232 = (bf16[2,8,128,512]{3,2,1,0:T(8,128)(2,1)}, bf16[2,8,128,512]{3,2,1,0:T(8,128)(2,1)}, bf16[2,8,64,1024]{3,2,1,0:T(8,128)(2,1)}, bf16[16,160,1024]{2,1,0:T(8,128)(2,1)}) custom-call(bf16[2,128,512]{2,1,0:T(8,128)(2,1)} %refs_0_.3, bf16[2,128,512]{2,1,0:T(8,128)(2,1)} %refs_1_.3, bf16[2,64,1024]{2,1,0:T(8,128)(2,1)} %refs_2_.3, ...), custom_call_target="tpu_custom_call" | custom-call | tf_op jit(solution)/shard_map/pallas_call | solution.py:431
  131.6 4.3 %fusion.121 = (f32[16,160]{1,0:T(8,128)S(1)}, f32[16,32,160]{2,1,0:T(8,128)S(1)}) fusion(bf16[16,160,1024]{2,1,0:T(8,128)(2,1)} %get-tuple-element.46, bf16[1024,128]{1,0:T(8,128)(2,1)S(1)} %bitcast.199, bf16[16,32,256]{2,1,0:T(8,128)(2,1)} %get-tuple-element.47), kind=kOutput, calls=%fused_computation.184 | convolution fusion | flops 168015360 | bytes 6006784 | tf_op jit(solution)/shard_map/de,std->set/dot_general | solution.py:862
  136.0 0.9 divide_multiply_fusion
  137.1 3.7 convert_bitcast_fusion.1
  140.9 0.7 copy.119
  141.6 0.9 copy-done.14
  142.5 2.3 fusion.123
  144.8 5.5 %multiply_convert_fusion = (bf16[2,1024,512]{2,1,0:T(8,128)(2,1)}, f32[2,1024,512]{2,1,0:T(8,128)}) fusion(f32[2,1024,512]{2,1,0:T(8,128)S(1)} %fusion.123, bf16[2,1024,1024]{2,1,0:T(8,128)(2,1)S(1)} %bitcast.205, bf16[2,1024,512]{2,1,0:T(8,128)(2,1)S(1)} %bitcast.216), kind=kOutput, calls=%fused_computation.18 | convolution fusion | flops 2153775104 | bytes 16777216 | tf_op jit(solution)/shard_map/jrd,jdf->jrf/dot_general | solution.py:862
  150.3 1.2 convert_bitcast_fusion
  151.6 1.7 copy.122
  153.3 7.8 %fusion = (f32[2,1024]{1,0:T(2,128)S(1)}, bf16[2,1024,1024]{2,1,0:T(8,128)(2,1)}) fusion(f32[2,16,64,1024]{3,2,1,0:T(8,128)S(1)} %copy.122, bf16[2,1024,512]{2,1,0:T(8,128)(2,1)} %get-tuple-element.115, bf16[2,512,1024]{2,1,0:T(8,128)(2,1)S(1)} %bitcast.218), kind=kOutput, calls=%fused_computation.4 | convolution fusion | flops 2155870208 | bytes 16785408 | tf_op jit(solution)/shard_map/jrf,jfd->jrd/dot_general | solution.py:862
  161.2 1.3 fusion.20
  162.5 7.2 %fusion.1 = (bf16[2,1024,1024]{2,1,0:T(8,128)(2,1)}, bf16[2,1024,1024]{2,1,0:T(8,128)(2,1)S(1)}) fusion(bf16[2,1024,1024]{2,1,0:T(8,128)(2,1)} %get-tuple-element.118, f32[2,1024]{1,0:T(2,128)S(1)} %mul.280, f32[2,16,64,1024]{3,2,1,0:T(8,128)} %copy-done.3), kind=kLoop, calls=%fused_computation.5 | loop fusion | flops 10485760 | bytes 20979712 | tf_op jit(solution)/shard_map/convert_element_type | solution.py:965
  169.7 6.2 %multiply_convert_fusion.1 = (bf16[2,1024,512]{2,1,0:T(8,128)(2,1)S(1)}, bf16[2,1024,512]{2,1,0:T(8,128)(2,1)S(1)}) fusion(f32[2,1024,512]{2,1,0:T(8,128)} %copy-done.30, f32[2,1024,512]{2,1,0:T(8,128)} %get-tuple-element.116, bf16[2,1024,1024]{2,1,0:T(8,128)(2,1)S(1)} %get-tuple-element.101, bf16[2,512,1024]{2,1,0:T(8,128)(2,1)S(1)} %bitcast.219), kind=kOutput, calls=%fused_computation.19 | convolution fusion | flops 2161115136 | bytes 18874368 | tf_op jit(solution)/shard_map/jrd,jfd->jrf/dot_general | solution.py:862
  175.9 3.7 convolution_convert_fusion.6
  179.7 3.7 convolution_convert_fusion.5
  183.4 3.8 convolution_convert_fusion.4
  187.2 2.4 fusion.124
  189.6 2.4 add_convert_fusion
  192.0 3.9 bitcast_convert_fusion.1.refs_3_
  196.5 47.3 %shard_map.233 = (bf16[2,128,512]{2,1,0:T(8,128)(2,1)}, bf16[2,128,512]{2,1,0:T(8,128)(2,1)}, bf16[2,64,1024]{2,1,0:T(8,128)(2,1)}, f32[160,1024]{1,0:T(8,128)}, f32[16,8,256]{2,1,0:T(8,128)}) custom-call(bf16[2,8,128,512]{3,2,1,0:T(8,128)(2,1)} %bitcast.213, bf16[2,8,128,512]{3,2,1,0:T(8,128)(2,1)} %bitcast.214, bf16[2,8,64,1024]{3,2,1,0:T(8,128)(2,1)} %bitcast.215, ...), custom_call_target="tpu_custom_call" | custom-call | tf_op jit(solution)/shard_map/pallas_call | solution.py:431
  243.8 0.9 slice.106
  245.1 1.7 multiply_reduce_fusion
  246.9 1.2 subtract_add_fusion
  248.1 0.8 convolution_convert_fusion.7.g_ref
  248.9 12.0 %shard_map.234 = (f32[160,1024]{1,0:T(8,128)S(1)}, bf16[1280,512]{1,0:T(8,128)(2,1)S(1)}, bf16[1280,512]{1,0:T(8,128)(2,1)S(1)}) custom-call(bf16[160,1024]{1,0:T(8,128)(2,1)S(1)} %get-tuple-element.104.q_ref, bf16[1280,1024]{1,0:T(8,128)(2,1)} %bitcast.184, bf16[1280,1024]{1,0:T(8,128)(2,1)} %bitcast.185, ...), custom_call_target="tpu_custom_call" | custom-call | tf_op jit(solution)/shard_map/pallas_call | solution.py:805
  261.3 3.0 fusion.60
  264.3 2.2 convolution_convert_fusion.3
  266.5 2.1 convolution_convert_fusion.2
  268.6 20.8 %shard_map.235 = (bf16[2,80,512]{2,1,0:T(8,128)(2,1)}, bf16[2,80,512]{2,1,0:T(8,128)(2,1)}) custom-call(bf16[8,2,80,512]{3,2,1,0:T(8,128)(2,1)} %bitcast.188, bf16[8,2,80,512]{3,2,1,0:T(8,128)(2,1)} %bitcast.189), custom_call_target="tpu_custom_call" | custom-call | tf_op jit(solution)/shard_map/pallas_call | solution.py:431
  289.4 0.9 bitcast_convert_fusion.5
  290.6 1.1 fusion.71
  291.7 3.1 convolution_convert_fusion.1
  295.3 2.5 fusion.125
  297.8 1.8 convolution_add_fusion.1
  299.7 0.7 fusion.50
  301.1 1.0 maximum_maximum_fusion.refs_3_
  302.1 6.1 %bitcast_convert_fusion.refs_4_ = bf16[16,160,1024]{2,1,0:T(8,128)(2,1)} fusion(bf16[2,16,64,1024]{3,2,1,0:T(8,128)(2,1)} %bitcast.190, s32[16,2,160]{2,1,0:T(2,128)S(1)} %copy.118, pred[16,2,160]{2,1,0:T(4,128)(4,1)S(1)} %broadcast_compare_fusion), kind=kOutput, calls=%fused_computation.2 | convolution fusion | flops 674365440 | bytes 9462784 | tf_op jit(solution)/shard_map/sjct,jscd->std/dot_general | solution.py:862
  308.2 83.3 %shard_map.236 = (bf16[4,2,16,1024]{3,2,1,0:T(8,128)(2,1)}, bf16[4,2,16,1024]{3,2,1,0:T(8,128)(2,1)}, bf16[4,2,16,1024]{3,2,1,0:T(8,128)(2,1)}, f32[4,32,128]{2,1,0:T(8,128)}, f32[160,1024]{1,0:T(8,128)}) custom-call(bf16[8,2,64,1024]{3,2,1,0:T(8,128)(2,1)} %bitcast.196, bf16[8,2,64,1024]{3,2,1,0:T(8,128)(2,1)} %bitcast.197, ...), custom_call_target="tpu_custom_call" | custom-call | tf_op jit(solution)/shard_map/pallas_call | solution.py:431
  391.5 2.4 fusion.61
  393.9 1.0 fusion.120
  395.5 2.1 bitcast_convert_fusion.2
  397.7 0.8 fusion.115
  399.1 0.7 copy.147
  399.8 0.9 convert_element_type.306
  400.6 0.9 convert_element_type.307
  401.5 0.8 convert_element_type.308
  (120 shorter events, 8.5 us)
Async XLA Ops:
  53.5 5.6 %copy-start.4 = (bf16[1,160,1024]{2,1,0:T(8,128)(2,1)S(1)}, bf16[1,160,1024]{2,1,0:T(8,128)(2,1)}, u32[]{:S(2)}) copy-start(bf16[1,160,1024]{2,1,0:T(8,128)(2,1)} %param.14) | copy-start | bytes 983044
  53.5 5.6 %copy-start.21 = (bf16[8,128,512]{2,1,0:T(8,128)(2,1)S(1)}, bf16[8,128,512]{2,1,0:T(8,128)(2,1)}, u32[]{:S(2)}) copy-start(bf16[8,128,512]{2,1,0:T(8,128)(2,1)} %get-tuple-element.43) | copy-start | bytes 3145732
  55.9 3.7 copy-start.10
  59.1 19.4 %copy-start.11 = (f32[160,1024]{1,0:T(8,128)}, f32[160,1024]{1,0:T(8,128)S(1)}, u32[]{:S(2)}) copy-start(f32[160,1024]{1,0:T(8,128)S(1)} %get-tuple-element.103) | copy-start | bytes 1966084
  78.9 1.7 copy-start
  80.7 11.0 %copy-start.13 = (f32[1024,1]{1,0:T(8,128)S(1)}, f32[1024,1]{1,0:T(8,128)}, u32[]{:S(2)}) copy-start(f32[1024,1]{1,0:T(8,128)} %get-tuple-element.96) | copy-start | bytes 12292
  89.3 42.2 %copy-start.6 = (bf16[8,128,128]{2,1,0:T(8,128)(2,1)S(1)}, bf16[8,128,128]{2,1,0:T(8,128)(2,1)}, u32[]{:S(2)}) copy-start(bf16[8,128,128]{2,1,0:T(8,128)(2,1)} %get-tuple-element.40) | copy-start | bytes 786436
  140.9 1.6 copy-start.14
  141.6 3.2 copy-start.8
  142.5 2.4 copy-start.16
  142.5 7.9 %slice-start = ((s8[5242880]{0:T(1024)(128)(4,1)}), s8[4194304]{0:T(1024)(128)(4,1)S(1)}, s32[]{:S(2)}) async-start(s8[5242880]{0:T(1024)(128)(4,1)} %bitcast.202), calls=%async_computation | async-start | bytes 8388608
  144.8 5.5 %copy-start.30 = (f32[2,1024,512]{2,1,0:T(8,128)}, f32[2,1024,512]{2,1,0:T(8,128)S(1)}, u32[]{:S(2)}) copy-start(f32[2,1024,512]{2,1,0:T(8,128)S(1)} %fusion.123) | copy-start | bytes 12582916
  144.8 5.5 %slice-start.1 = ((s8[5242880]{0:T(1024)(128)(4,1)}), s8[1048576]{0:T(1024)(128)(4,1)S(1)}, s32[]{:S(2)}) async-start(s8[5242880]{0:T(1024)(128)(4,1)} %bitcast.202), calls=%async_computation.1 | async-start | bytes 2097152
  151.6 1.7 copy-start.18
  153.3 7.8 %copy-start.3 = (f32[2,16,64,1024]{3,2,1,0:T(8,128)}, f32[2,16,64,1024]{3,2,1,0:T(8,128)S(1)}, u32[]{:S(2)}) copy-start(f32[2,16,64,1024]{3,2,1,0:T(8,128)S(1)} %copy.122) | copy-start | bytes 25165828
  162.5 7.2 %copy-start.19 = (bf16[2,8,64,1024]{3,2,1,0:T(8,128)(2,1)S(1)}, bf16[2,8,64,1024]{3,2,1,0:T(8,128)(2,1)}, u32[]{:S(2)}) copy-start(bf16[2,8,64,1024]{3,2,1,0:T(8,128)(2,1)} %get-tuple-element.49) | copy-start | bytes 6291460
  169.7 6.2 %copy-start.9 = (bf16[2,16,64,1024]{3,2,1,0:T(8,128)(2,1)S(1)}, bf16[2,16,64,1024]{3,2,1,0:T(8,128)(2,1)}, u32[]{:S(2)}) copy-start(bf16[2,16,64,1024]{3,2,1,0:T(8,128)(2,1)} %copy-done.8) | copy-start | bytes 12582916
  179.7 3.7 copy-start.20
  183.4 3.8 copy-start.15
  187.2 2.4 copy-start.17
  196.5 48.2 %copy-start.7 = (bf16[160,1024]{1,0:T(8,128)(2,1)S(1)}, bf16[160,1024]{1,0:T(8,128)(2,1)}, u32[]{:S(2)}) copy-start(bf16[160,1024]{1,0:T(8,128)(2,1)} %multiply_convert_fusion.3.refs_3_) | copy-start | bytes 983044
  244.7 3.3 copy-start.5
  260.9 7.7 %copy-start.1 = (bf16[1280,512]{1,0:T(8,128)(2,1)}, bf16[1280,512]{1,0:T(8,128)(2,1)S(1)}, u32[]{:S(2)}) copy-start(bf16[1280,512]{1,0:T(8,128)(2,1)S(1)} %get-tuple-element.56) | copy-start | bytes 3932164
  260.9 7.7 %copy-start.2 = (bf16[1280,512]{1,0:T(8,128)(2,1)}, bf16[1280,512]{1,0:T(8,128)(2,1)S(1)}, u32[]{:S(2)}) copy-start(bf16[1280,512]{1,0:T(8,128)(2,1)S(1)} %get-tuple-element.57) | copy-start | bytes 3932164
  266.5 24.1 %copy-start.12 = (f32[160,1024]{1,0:T(8,128)S(1)}, f32[160,1024]{1,0:T(8,128)}, u32[]{:S(2)}) copy-start(f32[160,1024]{1,0:T(8,128)} %copy-done.11) | copy-start | bytes 1966084
  291.7 3.1 copy-start.23
  291.7 7.9 %copy-start.29 = (bf16[2,80,512]{2,1,0:T(8,128)(2,1)S(1)}, bf16[2,80,512]{2,1,0:T(8,128)(2,1)}, u32[]{:S(2)}) copy-start(bf16[2,80,512]{2,1,0:T(8,128)(2,1)} %get-tuple-element.59) | copy-start | bytes 491524
  295.3 4.4 %copy-start.22 = (bf16[8,128,512]{2,1,0:T(8,128)(2,1)S(1)}, bf16[8,128,512]{2,1,0:T(8,128)(2,1)}, u32[]{:S(2)}) copy-start(bf16[8,128,512]{2,1,0:T(8,128)(2,1)} %get-tuple-element.43) | copy-start | bytes 3145732
  391.4 6.2 %copy-start.28 = (bf16[4,2,16,1024]{3,2,1,0:T(8,128)(2,1)S(1)}, bf16[4,2,16,1024]{3,2,1,0:T(8,128)(2,1)}, u32[]{:S(2)}) copy-start(bf16[4,2,16,1024]{3,2,1,0:T(8,128)(2,1)} %get-tuple-element.63) | copy-start | bytes 786436
  391.4 7.6 %copy-start.24 = (f32[4,32,128]{2,1,0:T(8,128)S(1)}, f32[4,32,128]{2,1,0:T(8,128)}, u32[]{:S(2)}) copy-start(f32[4,32,128]{2,1,0:T(8,128)} %get-tuple-element.61) | copy-start | bytes 196612
  391.5 8.3 %copy-start.27 = (bf16[2,128,512]{2,1,0:T(8,128)(2,1)S(1)}, bf16[2,128,512]{2,1,0:T(8,128)(2,1)}, u32[]{:S(2)}) copy-start(bf16[2,128,512]{2,1,0:T(8,128)(2,1)} %get-tuple-element.65) | copy-start | bytes 786436
  391.5 9.2 %copy-start.26 = (bf16[2,128,512]{2,1,0:T(8,128)(2,1)S(1)}, bf16[2,128,512]{2,1,0:T(8,128)(2,1)}, u32[]{:S(2)}) copy-start(bf16[2,128,512]{2,1,0:T(8,128)(2,1)} %get-tuple-element.66) | copy-start | bytes 786436
  391.5 10.0 %copy-start.25 = (bf16[2,64,1024]{2,1,0:T(8,128)(2,1)S(1)}, bf16[2,64,1024]{2,1,0:T(8,128)(2,1)}, u32[]{:S(2)}) copy-start(bf16[2,64,1024]{2,1,0:T(8,128)(2,1)} %get-tuple-element.67) | copy-start | bytes 786436
